TPU v7x, 32 devices: a whole 2x2x4 slice. The times are simulated.
32 devices in a mesh: orb: 4 (over y, x), dom: 8 (over z, core).
Axes of the slice: x: 2, y: 2, z: 4, core: 2. Of those that a mesh axis runs over, the one named last changes fastest.
Arguments:
- orbitals: float32 [8, 40, 32, 128], P('orb', 'dom'), may hold values from -8 to 8
- face_metric: float32 [3, 40, 32, 128], P(None, 'dom'), may hold values from 0.2 to 2.2
- cross_metric: float32 [3, 40, 32, 128], P(None, 'dom'), may hold values from -0.25 to 0.25
- screen: float32 [40, 32, 128], P('dom'), may hold values from 0.1 to 0.4
- turn_orbital: int32 [4], replicated, may hold values from 0 to 7, as said below
Outputs:
- exchange: float32 [8, 40, 32, 128], P('orb', 'dom')
Inputs may be any that keep to these rules, and one draw needn't show every extreme that they name: `turn_orbital`: orbital numbers; both 0 and 7 occur, and a number may recur.
All inputs are finite; a program needn't handle non-finite values.
Results may differ from a plain program's by a relative error of at most 0.0001.
Values sent between devices are 32-bit elements; how exact they have to be, the bound alone decides.
No kernel may reach another device: no remote copies, remote signals or barrier semaphores. Data moves between devices by JAX's collectives and lax.ppermute only.
A program may use at most 64 MiB of HBM per device.

v0:
```python
import functools

import jax
import jax.numpy as jnp
from jax import lax
from jax.experimental import pallas as pl
from jax.experimental.pallas import tpu as pltpu
from jax.sharding import PartitionSpec as P

SWEEPS = 6
DEEP = SWEEPS - 1
BATCH = 4
WIDTH = 2
LANES = 128
TOP = 7
TALL = 32
LIMIT = 24 * 1024 * 1024


def padded_to_tile(rows):
    return -(-rows // 8) * 8


class Sizes:
    def __init__(self, groups, mine, planes, height, turns):
        self.groups, self.mine, self.planes, self.turns = groups, mine, planes, turns
        self.height = height
        self.orbs = groups * mine
        self.rows = height // groups
        self.window = self.rows + 2 * DEEP
        self.inner = self.window - 2
        self.span = planes + 2 * DEEP
        self.edge = DEEP - 1
        self.orb_rows = mine * planes * self.window
        self.orb_pack = padded_to_tile(self.orb_rows)
        self.metric_at = DEEP * self.window
        self.orb_at = self.metric_at + 6 * self.edge * self.inner
        self.side_pack = padded_to_tile(self.orb_at + self.orb_rows)


def pack_kernel(sz, orb_in, face_in, cross_in, screen_in, *refs):
    pieces = refs[: sz.groups]
    far_ref, near_ref, inv_ref, met_ref, orb_pad, met_pad = refs[sz.groups : sz.groups + 6]
    orb_ref, face_ref, cross_ref, screen_ref, sems = refs[sz.groups + 6 :]
    copies = [
        pltpu.make_async_copy(source, target, sems.at[i])
        for i, (source, target) in enumerate(
            ((orb_in, orb_ref), (face_in, face_ref), (cross_in, cross_ref), (screen_in, screen_ref))
        )
    ]
    for copy in copies:
        copy.start()
    group = lax.axis_index("orb")
    odd = lax.rem(lax.axis_index("dom"), 2)
    zeros = jnp.zeros((8, LANES), jnp.float32)
    end = 8 + sz.height
    for copy in copies:
        copy.wait()
    for p in range(sz.planes):
        for j in range(sz.mine):
            orb_pad[j, p, 0:8] = zeros
            orb_pad[j, p, end : end + 8] = zeros
            orb_pad[j, p, 8:end] = orb_ref[j, p]
        diag = screen_ref[p] + 2.0 * (face_ref[0, p] + face_ref[1, p] + face_ref[2, p])
        diag = diag + (jnp.abs(cross_ref[0, p]) + jnp.abs(cross_ref[1, p]) + jnp.abs(cross_ref[2, p]))
        met_pad[6, p, 8:end] = 1.0 / diag
        for c in range(3):
            met_pad[c, p, 8:end] = face_ref[c, p]
            met_pad[3 + c, p, 8:end] = 0.25 * cross_ref[c, p]
        for c in range(7):
            met_pad[c, p, 0:8] = zeros
            met_pad[c, p, end : end + 8] = zeros
    own = 8 + group * sz.rows - DEEP
    for s in range(sz.groups):
        first = 8 + jnp.bitwise_xor(group, s) * sz.rows - DEEP
        for j in range(sz.mine):
            for p in range(sz.planes):
                at = (j * sz.planes + p) * sz.window
                pieces[s][at : at + sz.window] = orb_pad[j, p, pl.ds(first, sz.window)]
    for ref, from_end in ((far_ref, odd), (near_ref, 1 - odd)):
        first_inv = from_end * (sz.planes - DEEP)
        first_met = from_end * (sz.planes - sz.edge)
        for p in range(DEEP):
            at = p * sz.window
            ref[at : at + sz.window] = met_pad[6, first_inv + p, pl.ds(own, sz.window)]
        for c in range(6):
            for p in range(sz.edge):
                at = sz.metric_at + (c * sz.edge + p) * sz.inner
                ref[at : at + sz.inner] = met_pad[c, first_met + p, pl.ds(own + 1, sz.inner)]
        for j in range(sz.mine):
            for p in range(DEEP):
                at = sz.orb_at + (j * DEEP + p) * sz.window
                ref[at : at + sz.window] = orb_pad[j, first_inv + p, pl.ds(own, sz.window)]
    for p in range(sz.planes):
        inv_ref[p, 0 : sz.window] = met_pad[6, p, pl.ds(own, sz.window)]
        for c in range(6):
            met_ref[c, p, 0 : sz.inner] = met_pad[c, p, pl.ds(own + 1, sz.inner)]


def list_pairs(sz, group, turn_ref, first_ref, second_ref, weight_ref, seen_ref, mult_ref):
    def slot_of(k):
        return jnp.bitwise_xor(k // sz.mine, group) * sz.mine + lax.rem(k, sz.mine)

    for i in range(sz.orbs):
        seen_ref[i] = 0
        mult_ref[i] = 0
    slots = [slot_of(turn_ref[t]) for t in range(sz.turns)]
    for k in slots:
        mult_ref[k] = mult_ref[k] + 1
    count = jnp.int32(0)
    for k in slots:
        fresh = 1 - seen_ref[k]
        times = mult_ref[k]

        def step(i, count, k=k, fresh=fresh, times=times):
            first_ref[count] = k
            second_ref[count] = i
            weight_ref[count] = times + mult_ref[i]
            return count + fresh * (1 - seen_ref[i])

        count = lax.fori_loop(0, sz.orbs, step, count)
        seen_ref[k] = 1
    for i in range(BATCH):
        first_ref[count + i] = 0
        second_ref[count + i] = 0
        weight_ref[count + i] = 0
    return count


def mirrored(odd, p, count):
    return p + odd * (count - 1 - 2 * p)


def start_turns(turn_in, turn_ref, sem):
    turns = pltpu.make_async_copy(turn_in, turn_ref, sem)
    turns.start()
    return turns


def fill_own(sz, odd, gathered, orbs):
    n, win = sz.planes, sz.window
    for p in range(n):
        to = DEEP + mirrored(odd, p, n)
        for s in range(sz.groups):
            for j in range(sz.mine):
                at = (j * n + p) * win
                orbs[s * sz.mine + j, to, TOP : TOP + win] = gathered[s][at : at + win]


def fill_side(sz, odd, base, side, rest, orbs):
    n, win = sz.planes, sz.window
    for p in range(DEEP):
        to = base + mirrored(odd, p, DEEP)
        for j in range(sz.mine):
            row = sz.orb_at + (j * DEEP + p) * win
            orbs[j, to, TOP : TOP + win] = side[row : row + win]
        for i in range(sz.orbs - sz.mine):
            row = (i // sz.mine) * sz.orb_pack + ((i % sz.mine) * n + p) * win
            orbs[sz.mine + i, to, TOP : TOP + win] = rest[row : row + win]


def fill_start(sz, orbs, inv, start, fields, firsts, seconds, planes):
    for p in planes:
        for r, size in ((TOP, 8), (TOP + 8, 8), (TOP + 16, 2)):
            scale = inv[p, r : r + size]
            for f in fields:
                start[f, p, r : r + size] = (
                    orbs[firsts[f], p, r : r + size] * orbs[seconds[f], p, r : r + size] * scale
                )


def sweep(source, start, coef, fields, row, planes, put):
    values = {}

    def fetch(f, p):
        up = source(f, p, row + 1)
        down = source(f, p, row - 1)
        return source(f, p, row), up - down, up + down

    for f in fields:
        values[f, planes[0] - 1] = fetch(f, planes[0] - 1)
        values[f, planes[0]] = fetch(f, planes[0])
    for p in planes:
        cs = [coef[c, p, row - 8 : row] for c in range(9)]
        for f in fields:
            values[f, p + 1] = fetch(f, p + 1)
            before, diff_before, _ = values.pop((f, p - 1))
            here, diff, both = values[f, p]
            after, diff_after, _ = values[f, p + 1]
            slope = after - before
            up = cs[3] * here + cs[4] * slope + cs[5] * diff
            down = cs[6] * here + cs[7] * slope + cs[8] * diff
            new = start[f, p, row : row + 8] + cs[0] * (after + before)
            new = new + cs[1] * both + cs[2] * (diff_after - diff_before)
            new = new + (pltpu.roll(up, LANES - 1, 1) + pltpu.roll(down, 1, 1))
            put(f, p, new)


HALVES = [range(f, f + WIDTH) for f in range(0, BATCH, WIDTH)]


def near_kernel(sz, slabs, turn_in, *refs):
    gathered = refs[: sz.groups]
    far_ref, near_ref, near_rest, inv_ref, met_ref, inv, coef, state = refs[sz.groups : sz.groups + 8]
    orbs, start, *refs = refs[sz.groups + 8 :]
    levels, (first_ref, second_ref, weight_ref, seen_ref, mult_ref, turn_ref, sem) = refs[: DEEP - 2], refs[DEEP - 2 :]
    turns = start_turns(turn_in, turn_ref, sem)
    group = lax.axis_index("orb")
    slab = lax.axis_index("dom")
    odd = lax.rem(slab, 2)
    inside = jnp.where((slab == 0) | (slab == slabs - 1), 0.0, 1.0)
    n, win = sz.planes, sz.window
    above = n + DEEP

    fill_own(sz, odd, gathered, orbs)
    fill_side(sz, odd, above, near_ref, near_rest, orbs)
    for p in range(n):
        to = DEEP + mirrored(odd, p, n)
        inv[to, TOP : TOP + win] = inv_ref[p, 0:win]
        for c in range(6):
            coef[c, to, 0 : sz.inner] = met_ref[c, p, 0 : sz.inner]
    for ref, base, first, live in ((far_ref, 0, 1, inside), (near_ref, above, 0, 1.0)):
        for p in range(DEEP):
            inv[base + mirrored(odd, p, DEEP), TOP : TOP + win] = ref[p * win : (p + 1) * win] * live
        for c in range(6):
            for p in range(sz.edge):
                row = sz.metric_at + (c * sz.edge + p) * sz.inner
                coef[c, base + first + mirrored(odd, p, sz.edge), 0 : sz.inner] = ref[row : row + sz.inner]

    lane = lax.broadcasted_iota(jnp.int32, (8, LANES), 1)
    side = (1 - 2 * odd).astype(jnp.float32)
    for p in range(1, sz.span - 1):
        for r in (0, 8):
            scale = inv[p, 8 + r : 16 + r]
            along = scale * side
            fx, fy, fz, xy, xz, yz = [
                coef[c, p, r : r + 8] * (along if c in (3, 4) else scale) for c in range(6)
            ]
            coef[0, p, r : r + 8] = fx
            coef[1, p, r : r + 8] = fy
            coef[2, p, r : r + 8] = xy
            for at, values, sign in ((3, fz, 1.0), (4, xz, -1.0), (5, yz, -1.0)):
                up = jnp.where(lane == 0, 0.0, pltpu.roll(values, 1, 1))
                down = jnp.where(lane == LANES - 1, 0.0, pltpu.roll(values, LANES - 1, 1))
                coef[at, p, r : r + 8] = up
                coef[at + 3, p, r : r + 8] = sign * down
    turns.wait()
    count = list_pairs(sz, group, turn_ref, first_ref, second_ref, weight_ref, seen_ref, mult_ref)

    def batch(index, carry):
        base = index * BATCH
        firsts = [first_ref[base + f] for f in range(BATCH)]
        seconds = [second_ref[base + f] for f in range(BATCH)]
        for fields in HALVES:
            fill_start(sz, orbs, inv, start, fields, firsts, seconds, range(DEEP, sz.span))
        for number in range(1, DEEP):
            for fields in HALVES:
                source = start if number == 1 else levels[number - 2]
                planes = list(range(DEEP + number, sz.span - number))
                for row in (8, 16):

                    def load(f, p, at, source=source):
                        return source[f, p, at : at + 8]

                    def put(f, p, new, row=row, number=number):
                        if number < DEEP - 1:
                            levels[number - 1][f, p, row : row + 8] = new
                        if p < DEEP + number + 2:
                            state[base + f, number - 1, p - DEEP - number, row : row + 8] = new

                    sweep(load, start, coef, fields, row, planes, put)
        return carry

    lax.fori_loop(0, (count + BATCH - 1) // BATCH, batch, 0)


def far_kernel(sz, turn_in, *refs):
    gathered = refs[: sz.groups]
    far_ref, far_rest, inv, coef, state = refs[sz.groups : sz.groups + 5]
    outs = refs[sz.groups + 5 : 2 * sz.groups + 5]
    orbs, total, start, *refs = refs[2 * sz.groups + 5 :]
    levels, (first_ref, second_ref, weight_ref, seen_ref, mult_ref, turn_ref, sem) = refs[: DEEP - 1], refs[DEEP - 1 :]
    turns = start_turns(turn_in, turn_ref, sem)
    group = lax.axis_index("orb")
    odd = lax.rem(lax.axis_index("dom"), 2)
    n = sz.planes
    fill_own(sz, odd, gathered, orbs)
    fill_side(sz, odd, 0, far_ref, far_rest, orbs)
    for i in range(sz.orbs):
        for p in range(n):
            total[i, p] = jnp.zeros((8, LANES), jnp.float32)
    turns.wait()
    count = list_pairs(sz, group, turn_ref, first_ref, second_ref, weight_ref, seen_ref, mult_ref)

    def batch(index, carry):
        base = index * BATCH
        firsts = [first_ref[base + f] for f in range(BATCH)]
        seconds = [second_ref[base + f] for f in range(BATCH)]
        weights = []
        for f in range(BATCH):
            w = weight_ref[base + f]
            weights.append(
                (w.astype(jnp.float32), jnp.where(firsts[f] == seconds[f], 0, w).astype(jnp.float32))
            )
        for fields in HALVES:
            fill_start(sz, orbs, inv, start, fields, firsts, seconds, range(DEEP + n))
        for number in range(1, DEEP + 1):
            for fields in HALVES:
                planes = list(range(number, number + n))

                def load(f, p, at, number=number):
                    if number == 1:
                        return start[f, p, at : at + 8]
                    if p < number - 1 + n:
                        return levels[number - 2][f, p, at : at + 8]
                    return state[base + f, number - 2, p - (number - 1 + n), at : at + 8]

                if number < DEEP:
                    for row in (8, 16):

                        def put(f, p, new, row=row, number=number):
                            levels[number - 1][f, p, row : row + 8] = new

                        sweep(load, start, coef, fields, row, planes, put)
                else:
                    row = TOP + DEEP

                    def put(f, p, new, row=row):
                        a, b = firsts[f], seconds[f]
                        q = p - DEEP
                        total[a, q] = total[a, q] + (weights[f][0] * new) * orbs[b, p, row : row + 8]
                        total[b, q] = total[b, q] + (weights[f][1] * new) * orbs[a, p, row : row + 8]

                    sweep(load, start, coef, fields, row, planes, put)
        return carry

    lax.fori_loop(0, (count + BATCH - 1) // BATCH, batch, 0)

    for s in range(sz.groups):
        for j in range(sz.mine):
            for p in range(n):
                outs[s][j, p] = total[s * sz.mine + j, mirrored(odd, p, n), 0 : sz.rows]


def unpack_kernel(sz, *refs):
    blocks, out_ref = refs[: sz.groups], refs[sz.groups]
    group = lax.axis_index("orb")
    for s in range(sz.groups):
        first = jnp.bitwise_xor(group, s) * sz.rows
        if sz.rows % 8 == 0:
            first = pl.multiple_of(first, 8)
        for j in range(sz.mine):
            for p in range(sz.planes):
                out_ref[j, p, pl.ds(first, sz.rows)] = blocks[s][j, p]


def body(groups, slabs, orbitals, face_metric, cross_metric, screen, turn_orbital):
    mine, planes, height, lanes = orbitals.shape
    sz = Sizes(groups, mine, planes, height, turn_orbital.shape[0])
    f32 = jnp.float32
    vmem = pl.BlockSpec(memory_space=pltpu.VMEM)
    hbm = pl.BlockSpec(memory_space=pltpu.HBM)
    params = pltpu.CompilerParams(vmem_limit_bytes=LIMIT)

    packed = pl.pallas_call(
        functools.partial(pack_kernel, sz),
        out_shape=[jax.ShapeDtypeStruct((sz.orb_pack, lanes), f32)] * groups
        + [jax.ShapeDtypeStruct((sz.side_pack, lanes), f32)] * 2
        + [
            jax.ShapeDtypeStruct((planes, 24, lanes), f32),
            jax.ShapeDtypeStruct((6, planes, 16, lanes), f32),
        ],
        in_specs=[hbm] * 4,
        out_specs=[vmem] * (groups + 4),
        scratch_shapes=[
            pltpu.VMEM((mine, planes, height + 16, lanes), f32),
            pltpu.VMEM((7, planes, height + 16, lanes), f32),
            pltpu.VMEM((mine, planes, height, lanes), f32),
            pltpu.VMEM((3, planes, height, lanes), f32),
            pltpu.VMEM((3, planes, height, lanes), f32),
            pltpu.VMEM((planes, height, lanes), f32),
            pltpu.SemaphoreType.DMA((4,)),
        ],
        compiler_params=params,
        name="pack",
    )(*[pltpu.with_memory_space_constraint(x, pltpu.HBM) for x in (orbitals, face_metric, cross_metric, screen)])
    pieces = packed[:groups]
    far, near, inverse, metric = packed[groups:]

    def swap(x, s):
        return lax.ppermute(x, "orb", [(i, i ^ s) for i in range(groups)])

    to_near = [(i, i ^ 1) for i in range(slabs)]
    to_far = []
    for g in range(groups):
        to_far += [(g * slabs + i, g * slabs + ((i + 1) ^ 1) - 1) for i in range(1, slabs - 1)]
        to_far += [(g * slabs + i, (g ^ 1) * slabs + i) for i in (0, slabs - 1)]
    gathered = [pieces[0]] + [swap(pieces[s], s) for s in range(1, groups)]
    far_side = lax.ppermute(far, ("orb", "dom"), to_far)
    near_side = lax.ppermute(near, "dom", to_near)
    rest = jnp.concatenate(gathered[1:], axis=0)
    far_rest = lax.ppermute(rest, ("orb", "dom"), to_far)
    near_rest = lax.ppermute(rest, "dom", to_near)

    turns = sz.turns
    most = turns * sz.orbs - turns * (turns - 1) // 2
    most = -(-most // BATCH) * BATCH
    room = turns * sz.orbs + BATCH
    field = pltpu.VMEM((BATCH, sz.span, TALL, lanes), f32)
    orbital_windows = pltpu.VMEM((sz.orbs, sz.span, TALL, lanes), f32)
    lists = [
        pltpu.SMEM((room,), jnp.int32),
        pltpu.SMEM((room,), jnp.int32),
        pltpu.SMEM((room,), jnp.int32),
        pltpu.SMEM((sz.orbs,), jnp.int32),
        pltpu.SMEM((sz.orbs,), jnp.int32),
        pltpu.SMEM((turns,), jnp.int32),
        pltpu.SemaphoreType.DMA(()),
    ]
    which = pltpu.with_memory_space_constraint(turn_orbital, pltpu.HBM)
    points = sz.rows * planes * lanes
    inverse, coefs, state = pl.pallas_call(
        functools.partial(near_kernel, sz, slabs),
        out_shape=[
            jax.ShapeDtypeStruct((sz.span, TALL, lanes), f32),
            jax.ShapeDtypeStruct((9, sz.span, 16, lanes), f32),
            jax.ShapeDtypeStruct((most, DEEP - 1, 2, TALL, lanes), f32),
        ],
        in_specs=[hbm] + [vmem] * (groups + 5),
        out_specs=[vmem] * 3,
        scratch_shapes=[orbital_windows] + [field] * (DEEP - 1) + lists,
        compiler_params=params,
        cost_estimate=pl.CostEstimate(flops=200 * most * points, bytes_accessed=20_000_000, transcendentals=0),
        name="near",
    )(which, *gathered, far_side, near_side, near_rest, inverse, metric)
    shares = pl.pallas_call(
        functools.partial(far_kernel, sz),
        out_shape=[jax.ShapeDtypeStruct((mine, planes, sz.rows, lanes), f32)] * groups,
        in_specs=[hbm] + [vmem] * (groups + 5),
        out_specs=[vmem] * groups,
        scratch_shapes=[orbital_windows, pltpu.VMEM((sz.orbs, planes, 8, lanes), f32)] + [field] * DEEP + lists,
        compiler_params=params,
        name="far",
    )(which, *gathered, far_side, far_rest, inverse, coefs, state)
    blocks = [shares[0]] + [swap(shares[s], s) for s in range(1, groups)]
    return pl.pallas_call(
        functools.partial(unpack_kernel, sz),
        out_shape=jax.ShapeDtypeStruct((mine, planes, height, lanes), f32),
        in_specs=[vmem] * groups,
        out_specs=vmem,
        compiler_params=params,
        name="unpack",
    )(*blocks)


def solution(mesh):
    in_specs = (
        P("orb", "dom", None, None),
        P(None, "dom", None, None),
        P(None, "dom", None, None),
        P("dom", None, None),
        P(),
    )
    out_specs = P("orb", "dom", None, None)
    return jax.shard_map(
        functools.partial(body, mesh.shape["orb"], mesh.shape["dom"]),
        mesh=mesh,
        in_specs=in_specs,
        out_specs=out_specs,
        check_vma=False,
    )
```

profile of v0, /device:TPU:0, one launch (start us, length us, event | category | flops | bytes accessed | tf_op | source)
XLA Modules:
  0.0 37.6 jit_solution(13260510480103589799)
XLA Ops:
  0.0 1.4 %pack.1 = (f32[184,128]{1,0:T(8,128)S(1)}, f32[184,128]{1,0:T(8,128)S(1)}, f32[184,128]{1,0:T(8,128)S(1)}, f32[184,128]{1,0:T(8,128)S(1)}, f32[656,128]{1,0:T(8,...) custom-call(f32[2,5,32,128]{3,2,1,0:T(8,128)} %orb_in.1, ...), custom_call_target="tpu_custom_call" | custom-call | tf_op jit(solution)/shard_map/pack/pallas_call | solution.py:365
  1.4 3.0 %collective-permute-start = (f32[184,128]{1,0:T(8,128)S(1)}, f32[184,128]{1,0:T(8,128)S(1)}, u32[]{:S(2)}, u32[]{:S(2)}) collective-permute-start(f32[184,128]{1,0:T(8,128)S(1)} %get-tuple-element.21), channel_id=1, source_target_pairs={{0,8},{8,0},{16,24},{24,16},{1,9},{9,1},{17,25},{25,17},{2,10},{10... | collective-permute-start | bytes 282632 | tf_op jit(solution)/shard_map/ppermute | solution.py:391
  4.4 1.5 %collective-permute-start.1 = (f32[184,128]{1,0:T(8,128)S(1)}, f32[184,128]{1,0:T(8,128)S(1)}, u32[]{:S(2)}, u32[]{:S(2)}) collective-permute-start(f32[184,128]{1,0:T(8,128)S(1)} %get-tuple-element.22), channel_id=1, source_target_pairs={{0,16},{8,24},{16,0},{24,8},{1,17},{9,25},{17,1},{25,9},{2,18},{10... | collective-permute-start | bytes 282632 | tf_op jit(solution)/shard_map/ppermute | solution.py:391
  5.9 0.0 collective-permute-start.2
  6.0 1.9 %collective-permute-start.3 = (f32[656,128]{1,0:T(8,128)S(1)}, f32[656,128]{1,0:T(8,128)S(1)}, u32[]{:S(2)}, u32[]{:S(2)}) collective-permute-start(f32[656,128]{1,0:T(8,128)S(1)} %get-tuple-element.24), channel_id=1, source_target_pairs={{1,2},{2,1},{3,4},{4,3},{5,6},{6,5},{0,8},{7,15},{9,10},{10,9},{11... | collective-permute-start | bytes 1007624 | tf_op jit(solution)/shard_map/ppermute | solution.py:399
  7.9 0.2 collective-permute-start.5
  8.1 0.0 collective-permute-done.refs_1_
  8.1 1.9 %collective-permute-done.1.refs_2_ = f32[184,128]{1,0:T(8,128)S(1)} collective-permute-done((f32[184,128]{1,0:T(8,128)S(1)}, f32[184,128]{1,0:T(8,128)S(1)}, u32[]{:S(2)}, u32[]{:S(2)}) %collective-permute-start.1) | collective-permute-done | bytes 94240 | tf_op jit(solution)/shard_map/ppermute | solution.py:391
  10.0 1.4 %collective-permute-done.2.refs_3_ = f32[184,128]{1,0:T(8,128)S(1)} collective-permute-done((f32[184,128]{1,0:T(8,128)S(1)}, f32[184,128]{1,0:T(8,128)S(1)}, u32[]{:S(2)}, u32[]{:S(2)}) %collective-permute-start.2) | collective-permute-done | bytes 94240 | tf_op jit(solution)/shard_map/ppermute | solution.py:391
  11.4 0.1 collective-permute-start.6
  11.5 0.6 %collective-permute-start.4 = (f32[552,128]{1,0:T(8,128)S(1)}, f32[552,128]{1,0:T(8,128)S(1)}, u32[]{:S(2)}, u32[]{:S(2)}) collective-permute-start(f32[552,128]{1,0:T(8,128)S(1)} %constant_dynamic-update-slice_fusion), channel_id=1, source_target_pairs={{1,2},{2,1},{3,4},{4,3},{5,6},{6,5},{0,8},{7,15},{9,10},{10,9},{11... | collective-permute-start | bytes 847880 | tf_op jit(solution)/shard_map/ppermute | solution.py:402
  12.1 2.0 %collective-permute-done.3.refs_4_ = f32[656,128]{1,0:T(8,128)S(1)} collective-permute-done((f32[656,128]{1,0:T(8,128)S(1)}, f32[656,128]{1,0:T(8,128)S(1)}, u32[]{:S(2)}, u32[]{:S(2)}) %collective-permute-start.3) | collective-permute-done | bytes 335904 | tf_op jit(solution)/shard_map/ppermute | solution.py:399
  14.1 0.0 collective-permute-done.5.refs_5_
  14.1 0.0 collective-permute-done.6.refs_6_
  14.1 6.9 %near.1 = (f32[15,32,128]{2,1,0:T(8,128)S(1)}, f32[9,15,16,128]{3,2,1,0:T(8,128)S(1)}, f32[28,4,2,32,128]{4,3,2,1,0:T(8,128)S(1)}) custom-call(s32[4]{0:T(128)} %turn_in.3, f32[184,128]{1,0:T(8,128)S(1)} %get-tuple-element.20.refs_0_, f32[184,128]{1,0:T(8,128)S(1)} %collective-permute-done.refs_1_, f32[184,128]{1,0:T(8,128)S(1)} %collective-permute-done.1.refs_2_, ...), custom_call_target="tpu_custom_call" | custom-call | flops 28672000 | bytes 20000000 | tf_op jit(solution)/shard_map/near/pallas_call | solution.py:422
  21.0 0.0 collective-permute-done.4.refs_5_
  21.0 8.5 %far.1 = (f32[2,5,8,128]{3,2,1,0:T(8,128)S(1)}, f32[2,5,8,128]{3,2,1,0:T(8,128)S(1)}, f32[2,5,8,128]{3,2,1,0:T(8,128)S(1)}, f32[2,5,8,128]{3,2,1,0:T(8,128)S(1)}) custom-call(s32[4]{0:T(128)} %turn_in.3, f32[184,128]{1,0:T(8,128)S(1)} %get-tuple-element.20.refs_0_, f32[184,128]{1,0:T(8,128)S(1)} %collective-permute-done.refs_1_, ...), custom_call_target="tpu_custom_call" | custom-call | tf_op jit(solution)/shard_map/far/pallas_call | solution.py:436
  29.5 1.0 %collective-permute-start.7 = (f32[2,5,8,128]{3,2,1,0:T(8,128)S(1)}, f32[2,5,8,128]{3,2,1,0:T(8,128)S(1)}, u32[]{:S(2)}, u32[]{:S(2)}) collective-permute-start(f32[2,5,8,128]{3,2,1,0:T(8,128)S(1)} %get-tuple-element.32), channel_id=1, source_target_pairs={{0,8},{8,0},{16,24},{24,16},{1,9},{9,1},{17,25},{25,17},{2,10},{10... | collective-permute-start | bytes 122888 | tf_op jit(solution)/shard_map/ppermute | solution.py:391
  30.5 1.5 %collective-permute-start.8 = (f32[2,5,8,128]{3,2,1,0:T(8,128)S(1)}, f32[2,5,8,128]{3,2,1,0:T(8,128)S(1)}, u32[]{:S(2)}, u32[]{:S(2)}) collective-permute-start(f32[2,5,8,128]{3,2,1,0:T(8,128)S(1)} %get-tuple-element.33), channel_id=1, source_target_pairs={{0,16},{8,24},{16,0},{24,8},{1,17},{9,25},{17,1},{25,9},{2,18},{10... | collective-permute-start | bytes 122888 | tf_op jit(solution)/shard_map/ppermute | solution.py:391
  32.1 1.0 %collective-permute-start.9 = (f32[2,5,8,128]{3,2,1,0:T(8,128)S(1)}, f32[2,5,8,128]{3,2,1,0:T(8,128)S(1)}, u32[]{:S(2)}, u32[]{:S(2)}) collective-permute-start(f32[2,5,8,128]{3,2,1,0:T(8,128)S(1)} %get-tuple-element.34), channel_id=1, source_target_pairs={{0,24},{8,16},{16,8},{24,0},{1,25},{9,17},{17,9},{25,1},{2,26},{10... | collective-permute-start | bytes 122888 | tf_op jit(solution)/shard_map/ppermute | solution.py:391
  33.1 0.5 %collective-permute-done.7.refs_1_ = f32[2,5,8,128]{3,2,1,0:T(8,128)S(1)} collective-permute-done((f32[2,5,8,128]{3,2,1,0:T(8,128)S(1)}, f32[2,5,8,128]{3,2,1,0:T(8,128)S(1)}, u32[]{:S(2)}, u32[]{:S(2)}) %collective-permute-start.7) | collective-permute-done | bytes 40992 | tf_op jit(solution)/shard_map/ppermute | solution.py:391
  33.6 1.0 %collective-permute-done.8.refs_2_ = f32[2,5,8,128]{3,2,1,0:T(8,128)S(1)} collective-permute-done((f32[2,5,8,128]{3,2,1,0:T(8,128)S(1)}, f32[2,5,8,128]{3,2,1,0:T(8,128)S(1)}, u32[]{:S(2)}, u32[]{:S(2)}) %collective-permute-start.8) | collective-permute-done | bytes 40992 | tf_op jit(solution)/shard_map/ppermute | solution.py:391
  34.5 2.4 %collective-permute-done.9.refs_3_ = f32[2,5,8,128]{3,2,1,0:T(8,128)S(1)} collective-permute-done((f32[2,5,8,128]{3,2,1,0:T(8,128)S(1)}, f32[2,5,8,128]{3,2,1,0:T(8,128)S(1)}, u32[]{:S(2)}, u32[]{:S(2)}) %collective-permute-start.9) | collective-permute-done | bytes 40992 | tf_op jit(solution)/shard_map/ppermute | solution.py:391
  37.0 0.7 %unpack.1 = f32[2,5,32,128]{3,2,1,0:T(8,128)} custom-call(f32[2,5,8,128]{3,2,1,0:T(8,128)S(1)} %get-tuple-element.31.refs_0_, f32[2,5,8,128]{3,2,1,0:T(8,128)S(1)} %collective-permute-done.7.refs_1_, f32[2,5,8,128]{3,2,1,0:T(8,128)S(1)} %collective-permute-done.8.refs_2_, f32[2,5,8,128]{3,2,1,0:T(8,128)S(1)} %collective-permute-done.9.refs_3_), custom_call_target="tpu_custom_call" | custom-call | tf_op jit(solution)/shard_map/unpack/pallas_call | solution.py:446
  (3 shorter events, 0.0 us)
Async XLA Ops:
  1.4 6.7 %collective-permute-start = (f32[184,128]{1,0:T(8,128)S(1)}, f32[184,128]{1,0:T(8,128)S(1)}, u32[]{:S(2)}, u32[]{:S(2)}) collective-permute-start(f32[184,128]{1,0:T(8,128)S(1)} %get-tuple-element.21), channel_id=1, source_target_pairs={{0,8},{8,0},{16,24},{24,16},{1,9},{9,1},{17,25},{25,17},{2,10},{10... | collective-permute-start | bytes 282632 | tf_op jit(solution)/shard_map/ppermute | solution.py:391
  4.4 5.6 %collective-permute-start.1 = (f32[184,128]{1,0:T(8,128)S(1)}, f32[184,128]{1,0:T(8,128)S(1)}, u32[]{:S(2)}, u32[]{:S(2)}) collective-permute-start(f32[184,128]{1,0:T(8,128)S(1)} %get-tuple-element.22), channel_id=1, source_target_pairs={{0,16},{8,24},{16,0},{24,8},{1,17},{9,25},{17,1},{25,9},{2,18},{10... | collective-permute-start | bytes 282632 | tf_op jit(solution)/shard_map/ppermute | solution.py:391
  5.9 5.5 %collective-permute-start.2 = (f32[184,128]{1,0:T(8,128)S(1)}, f32[184,128]{1,0:T(8,128)S(1)}, u32[]{:S(2)}, u32[]{:S(2)}) collective-permute-start(f32[184,128]{1,0:T(8,128)S(1)} %get-tuple-element.23), channel_id=1, source_target_pairs={{0,24},{8,16},{16,8},{24,0},{1,25},{9,17},{17,9},{25,1},{2,26},{10... | collective-permute-start | bytes 282632 | tf_op jit(solution)/shard_map/ppermute | solution.py:391
  6.0 8.1 %collective-permute-start.3 = (f32[656,128]{1,0:T(8,128)S(1)}, f32[656,128]{1,0:T(8,128)S(1)}, u32[]{:S(2)}, u32[]{:S(2)}) collective-permute-start(f32[656,128]{1,0:T(8,128)S(1)} %get-tuple-element.24), channel_id=1, source_target_pairs={{1,2},{2,1},{3,4},{4,3},{5,6},{6,5},{0,8},{7,15},{9,10},{10,9},{11... | collective-permute-start | bytes 1007624 | tf_op jit(solution)/shard_map/ppermute | solution.py:399
  7.9 6.2 %collective-permute-start.5 = (f32[656,128]{1,0:T(8,128)S(1)}, f32[656,128]{1,0:T(8,128)S(1)}, u32[]{:S(2)}, u32[]{:S(2)}) collective-permute-start(f32[656,128]{1,0:T(8,128)S(1)} %get-tuple-element.25), channel_id=1, source_target_pairs={{0,1},{1,0},{2,3},{3,2},{4,5},{5,4},{6,7},{7,6},{8,9},{9,8},{10,11... | collective-permute-start | bytes 1007624 | tf_op jit(solution)/shard_map/ppermute | solution.py:400
  11.4 2.7 %collective-permute-start.6 = (f32[552,128]{1,0:T(8,128)S(1)}, f32[552,128]{1,0:T(8,128)S(1)}, u32[]{:S(2)}, u32[]{:S(2)}) collective-permute-start(f32[552,128]{1,0:T(8,128)S(1)} %constant_dynamic-update-slice_fusion), channel_id=1, source_target_pairs={{0,1},{1,0},{2,3},{3,2},{4,5},{5,4},{6,7},{7,6},{8,9},{9,8},{10,11... | collective-permute-start | bytes 847880 | tf_op jit(solution)/shard_map/ppermute | solution.py:403
  11.5 9.5 %collective-permute-start.4 = (f32[552,128]{1,0:T(8,128)S(1)}, f32[552,128]{1,0:T(8,128)S(1)}, u32[]{:S(2)}, u32[]{:S(2)}) collective-permute-start(f32[552,128]{1,0:T(8,128)S(1)} %constant_dynamic-update-slice_fusion), channel_id=1, source_target_pairs={{1,2},{2,1},{3,4},{4,3},{5,6},{6,5},{0,8},{7,15},{9,10},{10,9},{11... | collective-permute-start | bytes 847880 | tf_op jit(solution)/shard_map/ppermute | solution.py:402
  29.5 4.1 %collective-permute-start.7 = (f32[2,5,8,128]{3,2,1,0:T(8,128)S(1)}, f32[2,5,8,128]{3,2,1,0:T(8,128)S(1)}, u32[]{:S(2)}, u32[]{:S(2)}) collective-permute-start(f32[2,5,8,128]{3,2,1,0:T(8,128)S(1)} %get-tuple-element.32), channel_id=1, source_target_pairs={{0,8},{8,0},{16,24},{24,16},{1,9},{9,1},{17,25},{25,17},{2,10},{10... | collective-permute-start | bytes 122888 | tf_op jit(solution)/shard_map/ppermute | solution.py:391
  30.5 4.0 %collective-permute-start.8 = (f32[2,5,8,128]{3,2,1,0:T(8,128)S(1)}, f32[2,5,8,128]{3,2,1,0:T(8,128)S(1)}, u32[]{:S(2)}, u32[]{:S(2)}) collective-permute-start(f32[2,5,8,128]{3,2,1,0:T(8,128)S(1)} %get-tuple-element.33), channel_id=1, source_target_pairs={{0,16},{8,24},{16,0},{24,8},{1,17},{9,25},{17,1},{25,9},{2,18},{10... | collective-permute-start | bytes 122888 | tf_op jit(solution)/shard_map/ppermute | solution.py:391
  32.1 4.9 %collective-permute-start.9 = (f32[2,5,8,128]{3,2,1,0:T(8,128)S(1)}, f32[2,5,8,128]{3,2,1,0:T(8,128)S(1)}, u32[]{:S(2)}, u32[]{:S(2)}) collective-permute-start(f32[2,5,8,128]{3,2,1,0:T(8,128)S(1)} %get-tuple-element.34), channel_id=1, source_target_pairs={{0,24},{8,16},{16,8},{24,0},{1,25},{9,17},{17,9},{25,1},{2,26},{10... | collective-permute-start | bytes 122888 | tf_op jit(solution)/shard_map/ppermute | solution.py:391
where the time goes:
time: 37.8 us; the launch traced here: 37.6 us
  Pallas kernels  17.5 us (46%)
  starting transfers between devices  10.9 us (29%)
  waiting for transfers between devices  9.15 us (24%)
    pallas_call x1, Pallas kernels, body(): pl.pallas_call(functools.partial(far_kernel, sz), out_shape=[jax.ShapeDty...  8.49 us
    ppermute x6, starting transfers between devices, swap(): return lax.ppermute(x, 'orb', [(i, i ^ s) for i in range(groups)])  8.1 us
    ppermute x6, waiting for transfers between devices, swap(): return lax.ppermute(x, 'orb', [(i, i ^ s) for i in range(groups)])  7.17 us
    pallas_call x1, Pallas kernels, body(): pl.pallas_call(functools.partial(near_kernel, sz, slabs), out_shape=[jax....  6.89 us
    ppermute x1, waiting for transfers between devices, body(): far_side = lax.ppermute(far, ('orb', 'dom'), to_far)  1.98 us
    ppermute x1, starting transfers between devices, body(): far_side = lax.ppermute(far, ('orb', 'dom'), to_far)  1.95 us
    pallas_call x1, Pallas kernels, body(): pl.pallas_call(functools.partial(pack_kernel, sz), out_shape=[jax.ShapeDt...  1.41 us
  transfers between devices with their start and end apart: 10, of which 6 were waited for; matrix products, arithmetic and copies ran while one was open for 0% of the time, Pallas kernels for 18%

commit v1 on v0

--- a/solution.py
+++ b/solution.py
@@ -9,8 +9,8 @@
 
 SWEEPS = 6
 DEEP = SWEEPS - 1
-BATCH = 4
-WIDTH = 2
+PARTS = (range(0, 2), range(2, 4), range(4, 7))
+BATCH = PARTS[-1][-1] + 1
 LANES = 128
 TOP = 7
 TALL = 32
@@ -26,6 +26,7 @@
         self.groups, self.mine, self.planes, self.turns = groups, mine, planes, turns
         self.height = height
         self.orbs = groups * mine
+        self.routes = [0] + sorted(range(1, groups), key=lambda s: (-bin(s).count("1"), s))
         self.rows = height // groups
         self.window = self.rows + 2 * DEEP
         self.inner = self.window - 2
@@ -71,12 +72,12 @@
             met_pad[c, p, 0:8] = zeros
             met_pad[c, p, end : end + 8] = zeros
     own = 8 + group * sz.rows - DEEP
-    for s in range(sz.groups):
+    for i, s in enumerate(sz.routes):
         first = 8 + jnp.bitwise_xor(group, s) * sz.rows - DEEP
         for j in range(sz.mine):
             for p in range(sz.planes):
                 at = (j * sz.planes + p) * sz.window
-                pieces[s][at : at + sz.window] = orb_pad[j, p, pl.ds(first, sz.window)]
+                pieces[i][at : at + sz.window] = orb_pad[j, p, pl.ds(first, sz.window)]
     for ref, from_end in ((far_ref, odd), (near_ref, 1 - odd)):
         first_inv = from_end * (sz.planes - DEEP)
         first_met = from_end * (sz.planes - sz.edge)
@@ -141,10 +142,10 @@
     n, win = sz.planes, sz.window
     for p in range(n):
         to = DEEP + mirrored(odd, p, n)
-        for s in range(sz.groups):
+        for i, s in enumerate(sz.routes):
             for j in range(sz.mine):
                 at = (j * n + p) * win
-                orbs[s * sz.mine + j, to, TOP : TOP + win] = gathered[s][at : at + win]
+                orbs[s * sz.mine + j, to, TOP : TOP + win] = gathered[i][at : at + win]
 
 
 def fill_side(sz, odd, base, side, rest, orbs):
@@ -154,9 +155,10 @@
         for j in range(sz.mine):
             row = sz.orb_at + (j * DEEP + p) * win
             orbs[j, to, TOP : TOP + win] = side[row : row + win]
-        for i in range(sz.orbs - sz.mine):
-            row = (i // sz.mine) * sz.orb_pack + ((i % sz.mine) * n + p) * win
-            orbs[sz.mine + i, to, TOP : TOP + win] = rest[row : row + win]
+        for i, s in enumerate(sz.routes[1:]):
+            for j in range(sz.mine):
+                row = i * sz.orb_pack + (j * n + p) * win
+                orbs[s * sz.mine + j, to, TOP : TOP + win] = rest[row : row + win]
 
 
 def fill_start(sz, orbs, inv, start, fields, firsts, seconds, planes):
@@ -164,7 +166,7 @@
         for r, size in ((TOP, 8), (TOP + 8, 8), (TOP + 16, 2)):
             scale = inv[p, r : r + size]
             for f in fields:
-                start[f, p, r : r + size] = (
+                start[f - fields[0], p, r : r + size] = (
                     orbs[firsts[f], p, r : r + size] * orbs[seconds[f], p, r : r + size] * scale
                 )
 
@@ -190,20 +192,18 @@
             slope = after - before
             up = cs[3] * here + cs[4] * slope + cs[5] * diff
             down = cs[6] * here + cs[7] * slope + cs[8] * diff
-            new = start[f, p, row : row + 8] + cs[0] * (after + before)
+            new = start[f - fields[0], p, row : row + 8] + cs[0] * (after + before)
             new = new + cs[1] * both + cs[2] * (diff_after - diff_before)
-            new = new + (pltpu.roll(up, LANES - 1, 1) + pltpu.roll(down, 1, 1))
-            put(f, p, new)
-
-
-HALVES = [range(f, f + WIDTH) for f in range(0, BATCH, WIDTH)]
+            put(f, p, new + (pltpu.roll(up, LANES - 1, 1) + pltpu.roll(down, 1, 1)))
 
 
 def near_kernel(sz, slabs, turn_in, *refs):
     gathered = refs[: sz.groups]
     far_ref, near_ref, near_rest, inv_ref, met_ref, inv, coef, state = refs[sz.groups : sz.groups + 8]
-    orbs, start, *refs = refs[sz.groups + 8 :]
-    levels, (first_ref, second_ref, weight_ref, seen_ref, mult_ref, turn_ref, sem) = refs[: DEEP - 2], refs[DEEP - 2 :]
+    orbs, *refs = refs[sz.groups + 8 :]
+    starts, refs = refs[: len(PARTS)], refs[len(PARTS) :]
+    every = len(PARTS) * (DEEP - 2)
+    levels, (first_ref, second_ref, weight_ref, seen_ref, mult_ref, turn_ref, sem) = refs[:every], refs[every:]
     turns = start_turns(turn_in, turn_ref, sem)
     group = lax.axis_index("orb")
     slab = lax.axis_index("dom")
@@ -251,20 +251,21 @@
         base = index * BATCH
         firsts = [first_ref[base + f] for f in range(BATCH)]
         seconds = [second_ref[base + f] for f in range(BATCH)]
-        for fields in HALVES:
+        for fields, start in zip(PARTS, starts):
             fill_start(sz, orbs, inv, start, fields, firsts, seconds, range(DEEP, sz.span))
         for number in range(1, DEEP):
-            for fields in HALVES:
-                source = start if number == 1 else levels[number - 2]
+            for h, fields in enumerate(PARTS):
+                start, low = starts[h], fields[0]
+                source = start if number == 1 else levels[h * (DEEP - 2) + number - 2]
                 planes = list(range(DEEP + number, sz.span - number))
                 for row in (8, 16):
 
-                    def load(f, p, at, source=source):
-                        return source[f, p, at : at + 8]
-
-                    def put(f, p, new, row=row, number=number):
+                    def load(f, p, at, source=source, low=low):
+                        return source[f - low, p, at : at + 8]
+
+                    def put(f, p, new, row=row, number=number, low=low, h=h):
                         if number < DEEP - 1:
-                            levels[number - 1][f, p, row : row + 8] = new
+                            levels[h * (DEEP - 2) + number - 1][f - low, p, row : row + 8] = new
                         if p < DEEP + number + 2:
                             state[base + f, number - 1, p - DEEP - number, row : row + 8] = new
 
@@ -278,8 +279,10 @@
     gathered = refs[: sz.groups]
     far_ref, far_rest, inv, coef, state = refs[sz.groups : sz.groups + 5]
     outs = refs[sz.groups + 5 : 2 * sz.groups + 5]
-    orbs, total, start, *refs = refs[2 * sz.groups + 5 :]
-    levels, (first_ref, second_ref, weight_ref, seen_ref, mult_ref, turn_ref, sem) = refs[: DEEP - 1], refs[DEEP - 1 :]
+    orbs, total, *refs = refs[2 * sz.groups + 5 :]
+    starts, refs = refs[: len(PARTS)], refs[len(PARTS) :]
+    every = len(PARTS) * (DEEP - 1)
+    levels, (first_ref, second_ref, weight_ref, seen_ref, mult_ref, turn_ref, sem) = refs[:every], refs[every:]
     turns = start_turns(turn_in, turn_ref, sem)
     group = lax.axis_index("orb")
     odd = lax.rem(lax.axis_index("dom"), 2)
@@ -302,24 +305,25 @@
             weights.append(
                 (w.astype(jnp.float32), jnp.where(firsts[f] == seconds[f], 0, w).astype(jnp.float32))
             )
-        for fields in HALVES:
+        for fields, start in zip(PARTS, starts):
             fill_start(sz, orbs, inv, start, fields, firsts, seconds, range(DEEP + n))
         for number in range(1, DEEP + 1):
-            for fields in HALVES:
+            for h, fields in enumerate(PARTS):
+                start, low = starts[h], fields[0]
                 planes = list(range(number, number + n))
 
-                def load(f, p, at, number=number):
+                def load(f, p, at, number=number, start=start, low=low, h=h):
                     if number == 1:
-                        return start[f, p, at : at + 8]
+                        return start[f - low, p, at : at + 8]
                     if p < number - 1 + n:
-                        return levels[number - 2][f, p, at : at + 8]
+                        return levels[h * (DEEP - 1) + number - 2][f - low, p, at : at + 8]
                     return state[base + f, number - 2, p - (number - 1 + n), at : at + 8]
 
                 if number < DEEP:
                     for row in (8, 16):
 
-                        def put(f, p, new, row=row, number=number):
-                            levels[number - 1][f, p, row : row + 8] = new
+                        def put(f, p, new, row=row, number=number, low=low, h=h):
+                            levels[h * (DEEP - 1) + number - 1][f - low, p, row : row + 8] = new
 
                         sweep(load, start, coef, fields, row, planes, put)
                 else:
@@ -336,22 +340,22 @@
 
     lax.fori_loop(0, (count + BATCH - 1) // BATCH, batch, 0)
 
-    for s in range(sz.groups):
+    for i, s in enumerate(sz.routes):
         for j in range(sz.mine):
             for p in range(n):
-                outs[s][j, p] = total[s * sz.mine + j, mirrored(odd, p, n), 0 : sz.rows]
+                outs[i][j, p] = total[s * sz.mine + j, mirrored(odd, p, n), 0 : sz.rows]
 
 
 def unpack_kernel(sz, *refs):
     blocks, out_ref = refs[: sz.groups], refs[sz.groups]
     group = lax.axis_index("orb")
-    for s in range(sz.groups):
+    for i, s in enumerate(sz.routes):
         first = jnp.bitwise_xor(group, s) * sz.rows
         if sz.rows % 8 == 0:
             first = pl.multiple_of(first, 8)
         for j in range(sz.mine):
             for p in range(sz.planes):
-                out_ref[j, p, pl.ds(first, sz.rows)] = blocks[s][j, p]
+                out_ref[j, p, pl.ds(first, sz.rows)] = blocks[i][j, p]
 
 
 def body(groups, slabs, orbitals, face_metric, cross_metric, screen, turn_orbital):
@@ -395,7 +399,7 @@
     for g in range(groups):
         to_far += [(g * slabs + i, g * slabs + ((i + 1) ^ 1) - 1) for i in range(1, slabs - 1)]
         to_far += [(g * slabs + i, (g ^ 1) * slabs + i) for i in (0, slabs - 1)]
-    gathered = [pieces[0]] + [swap(pieces[s], s) for s in range(1, groups)]
+    gathered = [pieces[0]] + [swap(piece, s) for piece, s in zip(pieces[1:], sz.routes[1:])]
     far_side = lax.ppermute(far, ("orb", "dom"), to_far)
     near_side = lax.ppermute(near, "dom", to_near)
     rest = jnp.concatenate(gathered[1:], axis=0)
@@ -406,7 +410,7 @@
     most = turns * sz.orbs - turns * (turns - 1) // 2
     most = -(-most // BATCH) * BATCH
     room = turns * sz.orbs + BATCH
-    field = pltpu.VMEM((BATCH, sz.span, TALL, lanes), f32)
+    field = [pltpu.VMEM((len(fields), sz.span, TALL, lanes), f32) for fields in PARTS]
     orbital_windows = pltpu.VMEM((sz.orbs, sz.span, TALL, lanes), f32)
     lists = [
         pltpu.SMEM((room,), jnp.int32),
@@ -428,7 +432,7 @@
         ],
         in_specs=[hbm] + [vmem] * (groups + 5),
         out_specs=[vmem] * 3,
-        scratch_shapes=[orbital_windows] + [field] * (DEEP - 1) + lists,
+        scratch_shapes=[orbital_windows] + field + [x for x in field for _ in range(DEEP - 2)] + lists,
         compiler_params=params,
         cost_estimate=pl.CostEstimate(flops=200 * most * points, bytes_accessed=20_000_000, transcendentals=0),
         name="near",
@@ -438,11 +442,14 @@
         out_shape=[jax.ShapeDtypeStruct((mine, planes, sz.rows, lanes), f32)] * groups,
         in_specs=[hbm] + [vmem] * (groups + 5),
         out_specs=[vmem] * groups,
-        scratch_shapes=[orbital_windows, pltpu.VMEM((sz.orbs, planes, 8, lanes), f32)] + [field] * DEEP + lists,
+        scratch_shapes=[orbital_windows, pltpu.VMEM((sz.orbs, planes, 8, lanes), f32)]
+        + field
+        + [x for x in field for _ in range(DEEP - 1)]
+        + lists,
         compiler_params=params,
         name="far",
     )(which, *gathered, far_side, far_rest, inverse, coefs, state)
-    blocks = [shares[0]] + [swap(shares[s], s) for s in range(1, groups)]
+    blocks = [shares[0]] + [swap(share, s) for share, s in zip(shares[1:], sz.routes[1:])]
     return pl.pallas_call(
         functools.partial(unpack_kernel, sz),
         out_shape=jax.ShapeDtypeStruct((mine, planes, height, lanes), f32),

time: 37.8 us -> 36.7 us (0.971)
  waiting for transfers between devices: 9.15 us -> 7.18 us
  starting transfers between devices: 10.9 us -> 12 us
    ppermute x6, waiting for transfers between devices: 7.17 us -> 5.36 us  [swap(): return lax.ppermute(x, 'orb', [(i, i ^ s) for i in range(groups)])]
    ppermute x1, starting transfers between devices: 0.62 us -> 1.67 us  [body(): far_rest = lax.ppermute(rest, ('orb', 'dom'), to_far)]
  transfers between devices with their start and end apart: 10 -> 10, of which waited for: 6 -> 6; matrix products, arithmetic and copies ran while one was open for 0% -> 0% of each run, Pallas kernels for 18% -> 19%
where the time goes in v1:
time: 36.7 us; the launch traced here: 36.5 us
  Pallas kernels  17.3 us (47%)
  starting transfers between devices  12 us (33%)
  waiting for transfers between devices  7.18 us (20%)
    pallas_call x1, Pallas kernels, body(): pl.pallas_call(functools.partial(far_kernel, sz), out_shape=[jax.ShapeDty...  8.35 us
    ppermute x6, starting transfers between devices, swap(): return lax.ppermute(x, 'orb', [(i, i ^ s) for i in range(groups)])  8.15 us
    pallas_call x1, Pallas kernels, body(): pl.pallas_call(functools.partial(near_kernel, sz, slabs), out_shape=[jax....  6.82 us
    ppermute x6, waiting for transfers between devices, swap(): return lax.ppermute(x, 'orb', [(i, i ^ s) for i in range(groups)])  5.36 us
    ppermute x1, starting transfers between devices, body(): far_side = lax.ppermute(far, ('orb', 'dom'), to_far)  1.89 us
    ppermute x1, waiting for transfers between devices, body(): far_side = lax.ppermute(far, ('orb', 'dom'), to_far)  1.81 us
    ppermute x1, starting transfers between devices, body(): far_rest = lax.ppermute(rest, ('orb', 'dom'), to_far)  1.67 us
    pallas_call x1, Pallas kernels, body(): pl.pallas_call(functools.partial(pack_kernel, sz), out_shape=[jax.ShapeDt...  1.41 us
  transfers between devices with their start and end apart: 10, of which 6 were waited for; matrix products, arithmetic and copies ran while one was open for 0% of the time, Pallas kernels for 19%

profile of v1, /device:TPU:0, one launch (start us, length us, event | category | flops | bytes accessed | tf_op | source)
XLA Modules:
  0.0 36.5 jit_solution(17761360153900047685)
XLA Ops:
  0.0 1.4 %pack.1 = (f32[184,128]{1,0:T(8,128)S(1)}, f32[184,128]{1,0:T(8,128)S(1)}, f32[184,128]{1,0:T(8,128)S(1)}, f32[184,128]{1,0:T(8,128)S(1)}, f32[656,128]{1,0:T(8,...) custom-call(f32[2,5,32,128]{3,2,1,0:T(8,128)} %orb_in.1, ...), custom_call_target="tpu_custom_call" | custom-call | tf_op jit(solution)/shard_map/pack/pallas_call | solution.py:369
  1.4 4.0 %collective-permute-start = (f32[184,128]{1,0:T(8,128)S(1)}, f32[184,128]{1,0:T(8,128)S(1)}, u32[]{:S(2)}, u32[]{:S(2)}) collective-permute-start(f32[184,128]{1,0:T(8,128)S(1)} %get-tuple-element.21), channel_id=1, source_target_pairs={{0,24},{8,16},{16,8},{24,0},{1,25},{9,17},{17,9},{25,1},{2,26},{10... | collective-permute-start | bytes 282632 | tf_op jit(solution)/shard_map/ppermute | solution.py:395
  5.4 0.5 %collective-permute-start.1 = (f32[184,128]{1,0:T(8,128)S(1)}, f32[184,128]{1,0:T(8,128)S(1)}, u32[]{:S(2)}, u32[]{:S(2)}) collective-permute-start(f32[184,128]{1,0:T(8,128)S(1)} %get-tuple-element.22), channel_id=1, source_target_pairs={{0,8},{8,0},{16,24},{24,16},{1,9},{9,1},{17,25},{25,17},{2,10},{10... | collective-permute-start | bytes 282632 | tf_op jit(solution)/shard_map/ppermute | solution.py:395
  5.9 0.1 collective-permute-start.2
  6.0 1.9 %collective-permute-start.3 = (f32[656,128]{1,0:T(8,128)S(1)}, f32[656,128]{1,0:T(8,128)S(1)}, u32[]{:S(2)}, u32[]{:S(2)}) collective-permute-start(f32[656,128]{1,0:T(8,128)S(1)} %get-tuple-element.24), channel_id=1, source_target_pairs={{1,2},{2,1},{3,4},{4,3},{5,6},{6,5},{0,8},{7,15},{9,10},{10,9},{11... | collective-permute-start | bytes 1007624 | tf_op jit(solution)/shard_map/ppermute | solution.py:403
  7.9 0.2 collective-permute-start.5
  8.1 0.7 %collective-permute-done.refs_1_ = f32[184,128]{1,0:T(8,128)S(1)} collective-permute-done((f32[184,128]{1,0:T(8,128)S(1)}, f32[184,128]{1,0:T(8,128)S(1)}, u32[]{:S(2)}, u32[]{:S(2)}) %collective-permute-start) | collective-permute-done | bytes 94240 | tf_op jit(solution)/shard_map/ppermute | solution.py:395
  8.8 1.7 %collective-permute-done.1.refs_2_ = f32[184,128]{1,0:T(8,128)S(1)} collective-permute-done((f32[184,128]{1,0:T(8,128)S(1)}, f32[184,128]{1,0:T(8,128)S(1)}, u32[]{:S(2)}, u32[]{:S(2)}) %collective-permute-start.1) | collective-permute-done | bytes 94240 | tf_op jit(solution)/shard_map/ppermute | solution.py:395
  10.5 0.0 collective-permute-done.2.refs_3_
  10.5 0.1 collective-permute-start.6
  10.6 1.7 %collective-permute-start.4 = (f32[552,128]{1,0:T(8,128)S(1)}, f32[552,128]{1,0:T(8,128)S(1)}, u32[]{:S(2)}, u32[]{:S(2)}) collective-permute-start(f32[552,128]{1,0:T(8,128)S(1)} %constant_dynamic-update-slice_fusion), channel_id=1, source_target_pairs={{1,2},{2,1},{3,4},{4,3},{5,6},{6,5},{0,8},{7,15},{9,10},{10,9},{11... | collective-permute-start | bytes 847880 | tf_op jit(solution)/shard_map/ppermute | solution.py:406
  12.3 1.8 %collective-permute-done.3.refs_4_ = f32[656,128]{1,0:T(8,128)S(1)} collective-permute-done((f32[656,128]{1,0:T(8,128)S(1)}, f32[656,128]{1,0:T(8,128)S(1)}, u32[]{:S(2)}, u32[]{:S(2)}) %collective-permute-start.3) | collective-permute-done | bytes 335904 | tf_op jit(solution)/shard_map/ppermute | solution.py:403
  14.1 0.0 collective-permute-done.5.refs_5_
  14.1 0.0 collective-permute-done.6.refs_6_
  14.1 6.8 %near.1 = (f32[15,32,128]{2,1,0:T(8,128)S(1)}, f32[9,15,16,128]{3,2,1,0:T(8,128)S(1)}, f32[28,4,2,32,128]{4,3,2,1,0:T(8,128)S(1)}) custom-call(s32[4]{0:T(128)} %turn_in.3, f32[184,128]{1,0:T(8,128)S(1)} %get-tuple-element.20.refs_0_, f32[184,128]{1,0:T(8,128)S(1)} %collective-permute-done.refs_1_, f32[184,128]{1,0:T(8,128)S(1)} %collective-permute-done.1.refs_2_, ...), custom_call_target="tpu_custom_call" | custom-call | flops 28672000 | bytes 20000000 | tf_op jit(solution)/shard_map/near/pallas_call | solution.py:426
  20.9 0.0 collective-permute-done.4.refs_5_
  20.9 8.4 %far.1 = (f32[2,5,8,128]{3,2,1,0:T(8,128)S(1)}, f32[2,5,8,128]{3,2,1,0:T(8,128)S(1)}, f32[2,5,8,128]{3,2,1,0:T(8,128)S(1)}, f32[2,5,8,128]{3,2,1,0:T(8,128)S(1)}) custom-call(s32[4]{0:T(128)} %turn_in.3, f32[184,128]{1,0:T(8,128)S(1)} %get-tuple-element.20.refs_0_, f32[184,128]{1,0:T(8,128)S(1)} %collective-permute-done.refs_1_, ...), custom_call_target="tpu_custom_call" | custom-call | tf_op jit(solution)/shard_map/far/pallas_call | solution.py:440
  29.3 2.0 %collective-permute-start.7 = (f32[2,5,8,128]{3,2,1,0:T(8,128)S(1)}, f32[2,5,8,128]{3,2,1,0:T(8,128)S(1)}, u32[]{:S(2)}, u32[]{:S(2)}) collective-permute-start(f32[2,5,8,128]{3,2,1,0:T(8,128)S(1)} %get-tuple-element.32), channel_id=1, source_target_pairs={{0,24},{8,16},{16,8},{24,0},{1,25},{9,17},{17,9},{25,1},{2,26},{10... | collective-permute-start | bytes 122888 | tf_op jit(solution)/shard_map/ppermute | solution.py:395
  31.3 0.5 %collective-permute-start.8 = (f32[2,5,8,128]{3,2,1,0:T(8,128)S(1)}, f32[2,5,8,128]{3,2,1,0:T(8,128)S(1)}, u32[]{:S(2)}, u32[]{:S(2)}) collective-permute-start(f32[2,5,8,128]{3,2,1,0:T(8,128)S(1)} %get-tuple-element.33), channel_id=1, source_target_pairs={{0,8},{8,0},{16,24},{24,16},{1,9},{9,1},{17,25},{25,17},{2,10},{10... | collective-permute-start | bytes 122888 | tf_op jit(solution)/shard_map/ppermute | solution.py:395
  31.8 1.0 %collective-permute-start.9 = (f32[2,5,8,128]{3,2,1,0:T(8,128)S(1)}, f32[2,5,8,128]{3,2,1,0:T(8,128)S(1)}, u32[]{:S(2)}, u32[]{:S(2)}) collective-permute-start(f32[2,5,8,128]{3,2,1,0:T(8,128)S(1)} %get-tuple-element.34), channel_id=1, source_target_pairs={{0,16},{8,24},{16,0},{24,8},{1,17},{9,25},{17,1},{25,9},{2,18},{10... | collective-permute-start | bytes 122888 | tf_op jit(solution)/shard_map/ppermute | solution.py:395
  32.8 1.5 %collective-permute-done.7.refs_1_ = f32[2,5,8,128]{3,2,1,0:T(8,128)S(1)} collective-permute-done((f32[2,5,8,128]{3,2,1,0:T(8,128)S(1)}, f32[2,5,8,128]{3,2,1,0:T(8,128)S(1)}, u32[]{:S(2)}, u32[]{:S(2)}) %collective-permute-start.7) | collective-permute-done | bytes 40992 | tf_op jit(solution)/shard_map/ppermute | solution.py:395
  34.4 0.9 %collective-permute-done.8.refs_2_ = f32[2,5,8,128]{3,2,1,0:T(8,128)S(1)} collective-permute-done((f32[2,5,8,128]{3,2,1,0:T(8,128)S(1)}, f32[2,5,8,128]{3,2,1,0:T(8,128)S(1)}, u32[]{:S(2)}, u32[]{:S(2)}) %collective-permute-start.8) | collective-permute-done | bytes 40992 | tf_op jit(solution)/shard_map/ppermute | solution.py:395
  35.3 0.5 %collective-permute-done.9.refs_3_ = f32[2,5,8,128]{3,2,1,0:T(8,128)S(1)} collective-permute-done((f32[2,5,8,128]{3,2,1,0:T(8,128)S(1)}, f32[2,5,8,128]{3,2,1,0:T(8,128)S(1)}, u32[]{:S(2)}, u32[]{:S(2)}) %collective-permute-start.9) | collective-permute-done | bytes 40992 | tf_op jit(solution)/shard_map/ppermute | solution.py:395
  35.8 0.7 %unpack.1 = f32[2,5,32,128]{3,2,1,0:T(8,128)} custom-call(f32[2,5,8,128]{3,2,1,0:T(8,128)S(1)} %get-tuple-element.31.refs_0_, f32[2,5,8,128]{3,2,1,0:T(8,128)S(1)} %collective-permute-done.7.refs_1_, f32[2,5,8,128]{3,2,1,0:T(8,128)S(1)} %collective-permute-done.8.refs_2_, f32[2,5,8,128]{3,2,1,0:T(8,128)S(1)} %collective-permute-done.9.refs_3_), custom_call_target="tpu_custom_call" | custom-call | tf_op jit(solution)/shard_map/unpack/pallas_call | solution.py:453
  (3 shorter events, 0.0 us)
Async XLA Ops:
  1.4 7.4 %collective-permute-start = (f32[184,128]{1,0:T(8,128)S(1)}, f32[184,128]{1,0:T(8,128)S(1)}, u32[]{:S(2)}, u32[]{:S(2)}) collective-permute-start(f32[184,128]{1,0:T(8,128)S(1)} %get-tuple-element.21), channel_id=1, source_target_pairs={{0,24},{8,16},{16,8},{24,0},{1,25},{9,17},{17,9},{25,1},{2,26},{10... | collective-permute-start | bytes 282632 | tf_op jit(solution)/shard_map/ppermute | solution.py:395
  5.4 5.1 %collective-permute-start.1 = (f32[184,128]{1,0:T(8,128)S(1)}, f32[184,128]{1,0:T(8,128)S(1)}, u32[]{:S(2)}, u32[]{:S(2)}) collective-permute-start(f32[184,128]{1,0:T(8,128)S(1)} %get-tuple-element.22), channel_id=1, source_target_pairs={{0,8},{8,0},{16,24},{24,16},{1,9},{9,1},{17,25},{25,17},{2,10},{10... | collective-permute-start | bytes 282632 | tf_op jit(solution)/shard_map/ppermute | solution.py:395
  5.9 4.6 %collective-permute-start.2 = (f32[184,128]{1,0:T(8,128)S(1)}, f32[184,128]{1,0:T(8,128)S(1)}, u32[]{:S(2)}, u32[]{:S(2)}) collective-permute-start(f32[184,128]{1,0:T(8,128)S(1)} %get-tuple-element.23), channel_id=1, source_target_pairs={{0,16},{8,24},{16,0},{24,8},{1,17},{9,25},{17,1},{25,9},{2,18},{10... | collective-permute-start | bytes 282632 | tf_op jit(solution)/shard_map/ppermute | solution.py:395
  6.0 8.1 %collective-permute-start.3 = (f32[656,128]{1,0:T(8,128)S(1)}, f32[656,128]{1,0:T(8,128)S(1)}, u32[]{:S(2)}, u32[]{:S(2)}) collective-permute-start(f32[656,128]{1,0:T(8,128)S(1)} %get-tuple-element.24), channel_id=1, source_target_pairs={{1,2},{2,1},{3,4},{4,3},{5,6},{6,5},{0,8},{7,15},{9,10},{10,9},{11... | collective-permute-start | bytes 1007624 | tf_op jit(solution)/shard_map/ppermute | solution.py:403
  7.9 6.2 %collective-permute-start.5 = (f32[656,128]{1,0:T(8,128)S(1)}, f32[656,128]{1,0:T(8,128)S(1)}, u32[]{:S(2)}, u32[]{:S(2)}) collective-permute-start(f32[656,128]{1,0:T(8,128)S(1)} %get-tuple-element.25), channel_id=1, source_target_pairs={{0,1},{1,0},{2,3},{3,2},{4,5},{5,4},{6,7},{7,6},{8,9},{9,8},{10,11... | collective-permute-start | bytes 1007624 | tf_op jit(solution)/shard_map/ppermute | solution.py:404
  10.5 3.6 %collective-permute-start.6 = (f32[552,128]{1,0:T(8,128)S(1)}, f32[552,128]{1,0:T(8,128)S(1)}, u32[]{:S(2)}, u32[]{:S(2)}) collective-permute-start(f32[552,128]{1,0:T(8,128)S(1)} %constant_dynamic-update-slice_fusion), channel_id=1, source_target_pairs={{0,1},{1,0},{2,3},{3,2},{4,5},{5,4},{6,7},{7,6},{8,9},{9,8},{10,11... | collective-permute-start | bytes 847880 | tf_op jit(solution)/shard_map/ppermute | solution.py:407
  10.6 10.3 %collective-permute-start.4 = (f32[552,128]{1,0:T(8,128)S(1)}, f32[552,128]{1,0:T(8,128)S(1)}, u32[]{:S(2)}, u32[]{:S(2)}) collective-permute-start(f32[552,128]{1,0:T(8,128)S(1)} %constant_dynamic-update-slice_fusion), channel_id=1, source_target_pairs={{1,2},{2,1},{3,4},{4,3},{5,6},{6,5},{0,8},{7,15},{9,10},{10,9},{11... | collective-permute-start | bytes 847880 | tf_op jit(solution)/shard_map/ppermute | solution.py:406
  29.3 5.1 %collective-permute-start.7 = (f32[2,5,8,128]{3,2,1,0:T(8,128)S(1)}, f32[2,5,8,128]{3,2,1,0:T(8,128)S(1)}, u32[]{:S(2)}, u32[]{:S(2)}) collective-permute-start(f32[2,5,8,128]{3,2,1,0:T(8,128)S(1)} %get-tuple-element.32), channel_id=1, source_target_pairs={{0,24},{8,16},{16,8},{24,0},{1,25},{9,17},{17,9},{25,1},{2,26},{10... | collective-permute-start | bytes 122888 | tf_op jit(solution)/shard_map/ppermute | solution.py:395
  31.3 4.0 %collective-permute-start.8 = (f32[2,5,8,128]{3,2,1,0:T(8,128)S(1)}, f32[2,5,8,128]{3,2,1,0:T(8,128)S(1)}, u32[]{:S(2)}, u32[]{:S(2)}) collective-permute-start(f32[2,5,8,128]{3,2,1,0:T(8,128)S(1)} %get-tuple-element.33), channel_id=1, source_target_pairs={{0,8},{8,0},{16,24},{24,16},{1,9},{9,1},{17,25},{25,17},{2,10},{10... | collective-permute-start | bytes 122888 | tf_op jit(solution)/shard_map/ppermute | solution.py:395
  31.8 4.0 %collective-permute-start.9 = (f32[2,5,8,128]{3,2,1,0:T(8,128)S(1)}, f32[2,5,8,128]{3,2,1,0:T(8,128)S(1)}, u32[]{:S(2)}, u32[]{:S(2)}) collective-permute-start(f32[2,5,8,128]{3,2,1,0:T(8,128)S(1)} %get-tuple-element.34), channel_id=1, source_target_pairs={{0,16},{8,24},{16,0},{24,8},{1,17},{9,25},{17,1},{25,9},{2,18},{10... | collective-permute-start | bytes 122888 | tf_op jit(solution)/shard_map/ppermute | solution.py:395

commit v2 on v1

--- a/solution.py
+++ b/solution.py
@@ -98,44 +98,46 @@
             met_ref[c, p, 0 : sz.inner] = met_pad[c, p, pl.ds(own + 1, sz.inner)]
 
 
-def list_pairs(sz, group, turn_ref, first_ref, second_ref, weight_ref, seen_ref, mult_ref):
+def list_kernel(sz, turn_in, list_ref, seen_ref, mult_ref, turn_ref, sem):
+    turns = pltpu.make_async_copy(turn_in, turn_ref, sem)
+    turns.start()
+    group = lax.axis_index("orb")
+
     def slot_of(k):
         return jnp.bitwise_xor(k // sz.mine, group) * sz.mine + lax.rem(k, sz.mine)
 
     for i in range(sz.orbs):
         seen_ref[i] = 0
         mult_ref[i] = 0
+    turns.wait()
     slots = [slot_of(turn_ref[t]) for t in range(sz.turns)]
     for k in slots:
         mult_ref[k] = mult_ref[k] + 1
     count = jnp.int32(0)
+
+    def write(count, first, second, weight):
+        at = 1 + 3 * count
+        list_ref[at] = first
+        list_ref[at + 1] = second
+        list_ref[at + 2] = weight
+
     for k in slots:
         fresh = 1 - seen_ref[k]
         times = mult_ref[k]
 
         def step(i, count, k=k, fresh=fresh, times=times):
-            first_ref[count] = k
-            second_ref[count] = i
-            weight_ref[count] = times + mult_ref[i]
+            write(count, k, i, times + mult_ref[i])
             return count + fresh * (1 - seen_ref[i])
 
         count = lax.fori_loop(0, sz.orbs, step, count)
         seen_ref[k] = 1
     for i in range(BATCH):
-        first_ref[count + i] = 0
-        second_ref[count + i] = 0
-        weight_ref[count + i] = 0
-    return count
+        write(count + i, 0, 0, 0)
+    list_ref[0] = (count + BATCH - 1) // BATCH
 
 
 def mirrored(odd, p, count):
     return p + odd * (count - 1 - 2 * p)
-
-
-def start_turns(turn_in, turn_ref, sem):
-    turns = pltpu.make_async_copy(turn_in, turn_ref, sem)
-    turns.start()
-    return turns
 
 
 def fill_own(sz, odd, gathered, orbs):
@@ -197,39 +199,10 @@
             put(f, p, new + (pltpu.roll(up, LANES - 1, 1) + pltpu.roll(down, 1, 1)))
 
 
-def near_kernel(sz, slabs, turn_in, *refs):
-    gathered = refs[: sz.groups]
-    far_ref, near_ref, near_rest, inv_ref, met_ref, inv, coef, state = refs[sz.groups : sz.groups + 8]
-    orbs, *refs = refs[sz.groups + 8 :]
-    starts, refs = refs[: len(PARTS)], refs[len(PARTS) :]
-    every = len(PARTS) * (DEEP - 2)
-    levels, (first_ref, second_ref, weight_ref, seen_ref, mult_ref, turn_ref, sem) = refs[:every], refs[every:]
-    turns = start_turns(turn_in, turn_ref, sem)
-    group = lax.axis_index("orb")
-    slab = lax.axis_index("dom")
-    odd = lax.rem(slab, 2)
-    inside = jnp.where((slab == 0) | (slab == slabs - 1), 0.0, 1.0)
-    n, win = sz.planes, sz.window
-    above = n + DEEP
-
-    fill_own(sz, odd, gathered, orbs)
-    fill_side(sz, odd, above, near_ref, near_rest, orbs)
-    for p in range(n):
-        to = DEEP + mirrored(odd, p, n)
-        inv[to, TOP : TOP + win] = inv_ref[p, 0:win]
-        for c in range(6):
-            coef[c, to, 0 : sz.inner] = met_ref[c, p, 0 : sz.inner]
-    for ref, base, first, live in ((far_ref, 0, 1, inside), (near_ref, above, 0, 1.0)):
-        for p in range(DEEP):
-            inv[base + mirrored(odd, p, DEEP), TOP : TOP + win] = ref[p * win : (p + 1) * win] * live
-        for c in range(6):
-            for p in range(sz.edge):
-                row = sz.metric_at + (c * sz.edge + p) * sz.inner
-                coef[c, base + first + mirrored(odd, p, sz.edge), 0 : sz.inner] = ref[row : row + sz.inner]
-
+def prepare(odd, inv, coef, planes):
     lane = lax.broadcasted_iota(jnp.int32, (8, LANES), 1)
     side = (1 - 2 * odd).astype(jnp.float32)
-    for p in range(1, sz.span - 1):
+    for p in planes:
         for r in (0, 8):
             scale = inv[p, 8 + r : 16 + r]
             along = scale * side
@@ -244,13 +217,57 @@
                 down = jnp.where(lane == LANES - 1, 0.0, pltpu.roll(values, LANES - 1, 1))
                 coef[at, p, r : r + 8] = up
                 coef[at + 3, p, r : r + 8] = sign * down
-    turns.wait()
-    count = list_pairs(sz, group, turn_ref, first_ref, second_ref, weight_ref, seen_ref, mult_ref)
+
+
+def take_side(sz, odd, ref, base, first, inv, coef):
+    win = sz.window
+    for p in range(DEEP):
+        inv[base + mirrored(odd, p, DEEP), TOP : TOP + win] = ref[p * win : (p + 1) * win]
+    for c in range(6):
+        for p in range(sz.edge):
+            row = sz.metric_at + (c * sz.edge + p) * sz.inner
+            coef[c, base + first + mirrored(odd, p, sz.edge), 0 : sz.inner] = ref[row : row + sz.inner]
+
+
+def coefs_kernel(sz, near_ref, inv_ref, met_ref, inv, coef):
+    odd = lax.rem(lax.axis_index("dom"), 2)
+    n = sz.planes
+    for p in range(n):
+        to = mirrored(odd, p, n)
+        inv[to, TOP : TOP + sz.window] = inv_ref[p, 0 : sz.window]
+        for c in range(6):
+            coef[c, to, 0 : sz.inner] = met_ref[c, p, 0 : sz.inner]
+    take_side(sz, odd, near_ref, n, 0, inv, coef)
+    prepare(odd, inv, coef, range(n + sz.edge))
+
+
+class Planes:
+    def __init__(self, halo, others):
+        self.halo, self.others = halo, others
+
+    def __getitem__(self, at):
+        *lead, p, rows = at
+        ref, p = (self.halo, p) if p < DEEP else (self.others, p - DEEP)
+        return ref[(*lead, p, rows)]
+
+
+def near_kernel(sz, list_ref, *refs):
+    gathered = refs[: sz.groups]
+    near_ref, near_rest, inv, coef, state = refs[sz.groups : sz.groups + 5]
+    orbs, *refs = refs[sz.groups + 5 :]
+    starts, refs = refs[: len(PARTS)], refs[len(PARTS) :]
+    every = len(PARTS) * (DEEP - 2)
+    levels = refs[:every]
+    group = lax.axis_index("orb")
+    odd = lax.rem(lax.axis_index("dom"), 2)
+    inv, coef = Planes(None, inv), Planes(None, coef)
+    fill_own(sz, odd, gathered, orbs)
+    fill_side(sz, odd, sz.planes + DEEP, near_ref, near_rest, orbs)
 
     def batch(index, carry):
         base = index * BATCH
-        firsts = [first_ref[base + f] for f in range(BATCH)]
-        seconds = [second_ref[base + f] for f in range(BATCH)]
+        firsts = [list_ref[1 + 3 * (base + f)] for f in range(BATCH)]
+        seconds = [list_ref[2 + 3 * (base + f)] for f in range(BATCH)]
         for fields, start in zip(PARTS, starts):
             fill_start(sz, orbs, inv, start, fields, firsts, seconds, range(DEEP, sz.span))
         for number in range(1, DEEP):
@@ -272,36 +289,40 @@
                     sweep(load, start, coef, fields, row, planes, put)
         return carry
 
-    lax.fori_loop(0, (count + BATCH - 1) // BATCH, batch, 0)
-
-
-def far_kernel(sz, turn_in, *refs):
+    lax.fori_loop(0, list_ref[0], batch, 0)
+
+
+def far_kernel(sz, slabs, list_ref, *refs):
     gathered = refs[: sz.groups]
     far_ref, far_rest, inv, coef, state = refs[sz.groups : sz.groups + 5]
     outs = refs[sz.groups + 5 : 2 * sz.groups + 5]
-    orbs, total, *refs = refs[2 * sz.groups + 5 :]
+    orbs, total, inv_far, coef_far, *refs = refs[2 * sz.groups + 5 :]
     starts, refs = refs[: len(PARTS)], refs[len(PARTS) :]
     every = len(PARTS) * (DEEP - 1)
-    levels, (first_ref, second_ref, weight_ref, seen_ref, mult_ref, turn_ref, sem) = refs[:every], refs[every:]
-    turns = start_turns(turn_in, turn_ref, sem)
+    levels = refs[:every]
     group = lax.axis_index("orb")
-    odd = lax.rem(lax.axis_index("dom"), 2)
+    slab = lax.axis_index("dom")
+    odd = lax.rem(slab, 2)
     n = sz.planes
+    take_side(sz, odd, far_ref, 0, 1, inv_far, coef_far)
+    inside = jnp.where((slab == 0) | (slab == slabs - 1), 0.0, 1.0)
+    for p in range(DEEP):
+        inv_far[p, 0:TALL] = inv_far[p, 0:TALL] * inside
+    prepare(odd, inv_far, coef_far, range(1, DEEP))
+    inv, coef = Planes(inv_far, inv), Planes(coef_far, coef)
     fill_own(sz, odd, gathered, orbs)
     fill_side(sz, odd, 0, far_ref, far_rest, orbs)
     for i in range(sz.orbs):
         for p in range(n):
             total[i, p] = jnp.zeros((8, LANES), jnp.float32)
-    turns.wait()
-    count = list_pairs(sz, group, turn_ref, first_ref, second_ref, weight_ref, seen_ref, mult_ref)
 
     def batch(index, carry):
         base = index * BATCH
-        firsts = [first_ref[base + f] for f in range(BATCH)]
-        seconds = [second_ref[base + f] for f in range(BATCH)]
+        firsts = [list_ref[1 + 3 * (base + f)] for f in range(BATCH)]
+        seconds = [list_ref[2 + 3 * (base + f)] for f in range(BATCH)]
         weights = []
         for f in range(BATCH):
-            w = weight_ref[base + f]
+            w = list_ref[3 + 3 * (base + f)]
             weights.append(
                 (w.astype(jnp.float32), jnp.where(firsts[f] == seconds[f], 0, w).astype(jnp.float32))
             )
@@ -338,7 +359,7 @@
                     sweep(load, start, coef, fields, row, planes, put)
         return carry
 
-    lax.fori_loop(0, (count + BATCH - 1) // BATCH, batch, 0)
+    lax.fori_loop(0, list_ref[0], batch, 0)
 
     for i, s in enumerate(sz.routes):
         for j in range(sz.mine):
@@ -364,6 +385,7 @@
     f32 = jnp.float32
     vmem = pl.BlockSpec(memory_space=pltpu.VMEM)
     hbm = pl.BlockSpec(memory_space=pltpu.HBM)
+    smem = pl.BlockSpec(memory_space=pltpu.SMEM)
     params = pltpu.CompilerParams(vmem_limit_bytes=LIMIT)
 
     packed = pl.pallas_call(
@@ -402,53 +424,72 @@
     gathered = [pieces[0]] + [swap(piece, s) for piece, s in zip(pieces[1:], sz.routes[1:])]
     far_side = lax.ppermute(far, ("orb", "dom"), to_far)
     near_side = lax.ppermute(near, "dom", to_near)
-    rest = jnp.concatenate(gathered[1:], axis=0)
-    far_rest = lax.ppermute(rest, ("orb", "dom"), to_far)
-    near_rest = lax.ppermute(rest, "dom", to_near)
-
     turns = sz.turns
     most = turns * sz.orbs - turns * (turns - 1) // 2
     most = -(-most // BATCH) * BATCH
     room = turns * sz.orbs + BATCH
+    which = pltpu.with_memory_space_constraint(turn_orbital, pltpu.HBM)
+    points = sz.rows * planes * lanes
+    pairs = pl.pallas_call(
+        functools.partial(list_kernel, sz),
+        out_shape=jax.ShapeDtypeStruct((1 + 3 * room,), jnp.int32),
+        in_specs=[hbm],
+        out_specs=smem,
+        scratch_shapes=[
+            pltpu.SMEM((sz.orbs,), jnp.int32),
+            pltpu.SMEM((sz.orbs,), jnp.int32),
+            pltpu.SMEM((turns,), jnp.int32),
+            pltpu.SemaphoreType.DMA(()),
+        ],
+        compiler_params=params,
+        name="pairs",
+    )(which)
+    inverse, coefs = pl.pallas_call(
+        functools.partial(coefs_kernel, sz),
+        out_shape=[
+            jax.ShapeDtypeStruct((planes + DEEP, TALL, lanes), f32),
+            jax.ShapeDtypeStruct((9, planes + DEEP, 16, lanes), f32),
+        ],
+        in_specs=[vmem] * 3,
+        out_specs=[vmem] * 2,
+        compiler_params=params,
+        cost_estimate=pl.CostEstimate(flops=50 * points, bytes_accessed=2_500_000, transcendentals=0),
+        name="coefs",
+    )(near_side, inverse, metric)
+    *gathered, pairs, inverse, coefs = lax.optimization_barrier((*gathered, pairs, inverse, coefs))
+    rest = jnp.concatenate(gathered[1:], axis=0)
+    far_rest = lax.ppermute(rest, ("orb", "dom"), to_far)
+    near_rest = lax.ppermute(rest, "dom", to_near)
+
     field = [pltpu.VMEM((len(fields), sz.span, TALL, lanes), f32) for fields in PARTS]
     orbital_windows = pltpu.VMEM((sz.orbs, sz.span, TALL, lanes), f32)
-    lists = [
-        pltpu.SMEM((room,), jnp.int32),
-        pltpu.SMEM((room,), jnp.int32),
-        pltpu.SMEM((room,), jnp.int32),
-        pltpu.SMEM((sz.orbs,), jnp.int32),
-        pltpu.SMEM((sz.orbs,), jnp.int32),
-        pltpu.SMEM((turns,), jnp.int32),
-        pltpu.SemaphoreType.DMA(()),
-    ]
-    which = pltpu.with_memory_space_constraint(turn_orbital, pltpu.HBM)
-    points = sz.rows * planes * lanes
-    inverse, coefs, state = pl.pallas_call(
-        functools.partial(near_kernel, sz, slabs),
-        out_shape=[
-            jax.ShapeDtypeStruct((sz.span, TALL, lanes), f32),
-            jax.ShapeDtypeStruct((9, sz.span, 16, lanes), f32),
-            jax.ShapeDtypeStruct((most, DEEP - 1, 2, TALL, lanes), f32),
-        ],
-        in_specs=[hbm] + [vmem] * (groups + 5),
-        out_specs=[vmem] * 3,
-        scratch_shapes=[orbital_windows] + field + [x for x in field for _ in range(DEEP - 2)] + lists,
+    state = pl.pallas_call(
+        functools.partial(near_kernel, sz),
+        out_shape=jax.ShapeDtypeStruct((most, DEEP - 1, 2, TALL, lanes), f32),
+        in_specs=[smem] + [vmem] * (groups + 4),
+        out_specs=vmem,
+        scratch_shapes=[orbital_windows] + field + [x for x in field for _ in range(DEEP - 2)],
         compiler_params=params,
         cost_estimate=pl.CostEstimate(flops=200 * most * points, bytes_accessed=20_000_000, transcendentals=0),
         name="near",
-    )(which, *gathered, far_side, near_side, near_rest, inverse, metric)
+    )(pairs, *gathered, near_side, near_rest, inverse, coefs)
     shares = pl.pallas_call(
-        functools.partial(far_kernel, sz),
+        functools.partial(far_kernel, sz, slabs),
         out_shape=[jax.ShapeDtypeStruct((mine, planes, sz.rows, lanes), f32)] * groups,
-        in_specs=[hbm] + [vmem] * (groups + 5),
+        in_specs=[smem] + [vmem] * (groups + 5),
         out_specs=[vmem] * groups,
-        scratch_shapes=[orbital_windows, pltpu.VMEM((sz.orbs, planes, 8, lanes), f32)]
+        scratch_shapes=[
+            orbital_windows,
+            pltpu.VMEM((sz.orbs, planes, 8, lanes), f32),
+            pltpu.VMEM((DEEP, TALL, lanes), f32),
+            pltpu.VMEM((9, DEEP, 16, lanes), f32),
+        ]
         + field
         + [x for x in field for _ in range(DEEP - 1)]
-        + lists,
+       ,
         compiler_params=params,
         name="far",
-    )(which, *gathered, far_side, far_rest, inverse, coefs, state)
+    )(pairs, *gathered, far_side, far_rest, inverse, coefs, state)
     blocks = [shares[0]] + [swap(share, s) for share, s in zip(shares[1:], sz.routes[1:])]
     return pl.pallas_call(
         functools.partial(unpack_kernel, sz),

time: 36.7 us -> 31.4 us (0.86)
  Pallas kernels: 17.3 us -> 14.5 us
  waiting for transfers between devices: 7.18 us -> 4.92 us
    pallas_call x2 -> x4, Pallas kernels: 15.2 us -> 12.4 us  [the longest x1 5.79 us: body(): pl.pallas_call(functools.partial(far_kernel, sz, slabs), out_shape=[jax.S...]
    ppermute x1, waiting for transfers between devices: 1.81 us -> 0.01 us  [body(): far_side = lax.ppermute(far, ('orb', 'dom'), to_far)]
    ppermute x6, waiting for transfers between devices: 5.36 us -> 4.59 us  [swap(): return lax.ppermute(x, 'orb', [(i, i ^ s) for i in range(groups)])]
    ppermute x6, starting transfers between devices: 8.15 us -> 7.71 us  [swap(): return lax.ppermute(x, 'orb', [(i, i ^ s) for i in range(groups)])]
  transfers between devices with their start and end apart: 10 -> 10, of which waited for: 6 -> 5; matrix products, arithmetic and copies ran while one was open for 0% -> 0% of each run, Pallas kernels for 19% -> 21%
where the time goes in v2:
time: 31.4 us; the launch traced here: 31.3 us
  Pallas kernels  14.5 us (46%)
  starting transfers between devices  11.7 us (37%)
  waiting for transfers between devices  4.92 us (16%)
    ppermute x6, starting transfers between devices, swap(): return lax.ppermute(x, 'orb', [(i, i ^ s) for i in range(groups)])  7.71 us
    pallas_call x1, Pallas kernels, body(): pl.pallas_call(functools.partial(far_kernel, sz, slabs), out_shape=[jax.S...  5.79 us
    pallas_call x1, Pallas kernels, body(): pl.pallas_call(functools.partial(near_kernel, sz), out_shape=jax.ShapeDty...  4.76 us
    ppermute x6, waiting for transfers between devices, swap(): return lax.ppermute(x, 'orb', [(i, i ^ s) for i in range(groups)])  4.59 us
    ppermute x1, starting transfers between devices, body(): far_side = lax.ppermute(far, ('orb', 'dom'), to_far)  1.89 us
    pallas_call x1, Pallas kernels, body(): pl.pallas_call(functools.partial(list_kernel, sz), out_shape=jax.ShapeDty...  1.59 us
    ppermute x1, starting transfers between devices, body(): far_rest = lax.ppermute(rest, ('orb', 'dom'), to_far)  1.55 us
    pallas_call x1, Pallas kernels, body(): pl.pallas_call(functools.partial(pack_kernel, sz), out_shape=[jax.ShapeDt...  1.41 us
  transfers between devices with their start and end apart: 10, of which 5 were waited for; matrix products, arithmetic and copies ran while one was open for 0% of the time, Pallas kernels for 21%

profile of v2, /device:TPU:0, one launch (start us, length us, event | category | flops | bytes accessed | tf_op | source)
XLA Modules:
  0.0 31.3 jit_solution(12004843406795631207)
XLA Ops:
  0.0 1.4 %pack.1 = (f32[184,128]{1,0:T(8,128)S(1)}, f32[184,128]{1,0:T(8,128)S(1)}, f32[184,128]{1,0:T(8,128)S(1)}, f32[184,128]{1,0:T(8,128)S(1)}, f32[656,128]{1,0:T(8,...) custom-call(f32[2,5,32,128]{3,2,1,0:T(8,128)} %orb_in.1, ...), custom_call_target="tpu_custom_call" | custom-call | tf_op jit(solution)/shard_map/pack/pallas_call | solution.py:391
  1.4 0.5 %collective-permute-start.3 = (f32[656,128]{1,0:T(8,128)S(1)}, f32[656,128]{1,0:T(8,128)S(1)}, u32[]{:S(2)}, u32[]{:S(2)}) collective-permute-start(f32[656,128]{1,0:T(8,128)S(1)} %get-tuple-element.30), channel_id=1, source_target_pairs={{0,1},{1,0},{2,3},{3,2},{4,5},{5,4},{6,7},{7,6},{8,9},{9,8},{10,11... | collective-permute-start | bytes 1007624 | tf_op jit(solution)/shard_map/ppermute | solution.py:426
  1.9 3.5 %collective-permute-start = (f32[184,128]{1,0:T(8,128)S(1)}, f32[184,128]{1,0:T(8,128)S(1)}, u32[]{:S(2)}, u32[]{:S(2)}) collective-permute-start(f32[184,128]{1,0:T(8,128)S(1)} %get-tuple-element.27), channel_id=1, source_target_pairs={{0,24},{8,16},{16,8},{24,0},{1,25},{9,17},{17,9},{25,1},{2,26},{10... | collective-permute-start | bytes 282632 | tf_op jit(solution)/shard_map/ppermute | solution.py:417
  5.5 0.5 %collective-permute-start.1 = (f32[184,128]{1,0:T(8,128)S(1)}, f32[184,128]{1,0:T(8,128)S(1)}, u32[]{:S(2)}, u32[]{:S(2)}) collective-permute-start(f32[184,128]{1,0:T(8,128)S(1)} %get-tuple-element.28), channel_id=1, source_target_pairs={{0,8},{8,0},{16,24},{24,16},{1,9},{9,1},{17,25},{25,17},{2,10},{10... | collective-permute-start | bytes 282632 | tf_op jit(solution)/shard_map/ppermute | solution.py:417
  6.0 0.1 collective-permute-start.2
  6.1 1.9 %collective-permute-start.4 = (f32[656,128]{1,0:T(8,128)S(1)}, f32[656,128]{1,0:T(8,128)S(1)}, u32[]{:S(2)}, u32[]{:S(2)}) collective-permute-start(f32[656,128]{1,0:T(8,128)S(1)} %get-tuple-element.40), channel_id=1, source_target_pairs={{1,2},{2,1},{3,4},{4,3},{5,6},{6,5},{0,8},{7,15},{9,10},{10,9},{11... | collective-permute-start | bytes 1007624 | tf_op jit(solution)/shard_map/ppermute | solution.py:425
  8.0 1.6 %pairs.1.list_ref = s32[118]{0:T(128)S(1)} custom-call(s32[4]{0:T(128)} %turn_in.1), custom_call_target="tpu_custom_call" | custom-call | tf_op jit(solution)/shard_map/pairs/pallas_call | solution.py:433
  9.6 0.0 collective-permute-done.3.near_ref.refs_4_
  9.6 0.3 coefs.1
  9.9 1.2 %collective-permute-done.1.refs_2_ = f32[184,128]{1,0:T(8,128)S(1)} collective-permute-done((f32[184,128]{1,0:T(8,128)S(1)}, f32[184,128]{1,0:T(8,128)S(1)}, u32[]{:S(2)}, u32[]{:S(2)}) %collective-permute-start.1) | collective-permute-done | bytes 94240 | tf_op jit(solution)/shard_map/ppermute | solution.py:417
  11.1 0.1 collective-permute-start.6
  11.2 1.6 %collective-permute-start.5 = (f32[552,128]{1,0:T(8,128)S(1)}, f32[552,128]{1,0:T(8,128)S(1)}, u32[]{:S(2)}, u32[]{:S(2)}) collective-permute-start(f32[552,128]{1,0:T(8,128)S(1)} %constant_dynamic-update-slice_fusion), channel_id=1, source_target_pairs={{1,2},{2,1},{3,4},{4,3},{5,6},{6,5},{0,8},{7,15},{9,10},{10,9},{11... | collective-permute-start | bytes 847880 | tf_op jit(solution)/shard_map/ppermute | solution.py:461
  12.7 0.0 collective-permute-done.6.refs_5_
  12.7 4.8 %near.1.refs_8_ = f32[28,4,2,32,128]{4,3,2,1,0:T(8,128)S(1)} custom-call(s32[118]{0:T(128)S(1)} %pairs.1.list_ref, f32[184,128]{1,0:T(8,128)S(1)} %get-tuple-element.36.refs_0_, f32[184,128]{1,0:T(8,128)S(1)} %collective-permute-done.refs_1_, f32[184,128]{1,0:T(8,128)S(1)} %collective-permute-done.1.refs_2_, f32[184,128]{1,0:T(8,128)S(1)} %collective-permute-done.2.refs_3_, ...), custom_call_target="tpu_custom_call" | custom-call | flops 28672000 | bytes 20000000 | tf_op jit(solution)/shard_map/near/pallas_call | solution.py:466
  17.5 0.0 collective-permute-done.4.refs_4_
  17.5 0.3 %collective-permute-done.5.refs_5_ = f32[552,128]{1,0:T(8,128)S(1)} collective-permute-done((f32[552,128]{1,0:T(8,128)S(1)}, f32[552,128]{1,0:T(8,128)S(1)}, u32[]{:S(2)}, u32[]{:S(2)}) %collective-permute-start.5) | collective-permute-done | bytes 282656 | tf_op jit(solution)/shard_map/ppermute | solution.py:461
  17.8 5.8 %far.1 = (f32[2,5,8,128]{3,2,1,0:T(8,128)S(1)}, f32[2,5,8,128]{3,2,1,0:T(8,128)S(1)}, f32[2,5,8,128]{3,2,1,0:T(8,128)S(1)}, f32[2,5,8,128]{3,2,1,0:T(8,128)S(1)}) custom-call(s32[118]{0:T(128)S(1)} %pairs.1.list_ref, f32[184,128]{1,0:T(8,128)S(1)} %get-tuple-element.36.refs_0_, f32[184,128]{1,0:T(8,128)S(1)} %collective-permute-done.refs_1_, ...), custom_call_target="tpu_custom_call" | custom-call | tf_op jit(solution)/shard_map/far/pallas_call | solution.py:476
  23.6 2.5 %collective-permute-start.7 = (f32[2,5,8,128]{3,2,1,0:T(8,128)S(1)}, f32[2,5,8,128]{3,2,1,0:T(8,128)S(1)}, u32[]{:S(2)}, u32[]{:S(2)}) collective-permute-start(f32[2,5,8,128]{3,2,1,0:T(8,128)S(1)} %get-tuple-element.44), channel_id=1, source_target_pairs={{0,24},{8,16},{16,8},{24,0},{1,25},{9,17},{17,9},{25,1},{2,26},{10... | collective-permute-start | bytes 122888 | tf_op jit(solution)/shard_map/ppermute | solution.py:417
  26.1 0.5 %collective-permute-start.8 = (f32[2,5,8,128]{3,2,1,0:T(8,128)S(1)}, f32[2,5,8,128]{3,2,1,0:T(8,128)S(1)}, u32[]{:S(2)}, u32[]{:S(2)}) collective-permute-start(f32[2,5,8,128]{3,2,1,0:T(8,128)S(1)} %get-tuple-element.45), channel_id=1, source_target_pairs={{0,8},{8,0},{16,24},{24,16},{1,9},{9,1},{17,25},{25,17},{2,10},{10... | collective-permute-start | bytes 122888 | tf_op jit(solution)/shard_map/ppermute | solution.py:417
  26.6 0.6 %collective-permute-start.9 = (f32[2,5,8,128]{3,2,1,0:T(8,128)S(1)}, f32[2,5,8,128]{3,2,1,0:T(8,128)S(1)}, u32[]{:S(2)}, u32[]{:S(2)}) collective-permute-start(f32[2,5,8,128]{3,2,1,0:T(8,128)S(1)} %get-tuple-element.46), channel_id=1, source_target_pairs={{0,16},{8,24},{16,0},{24,8},{1,17},{9,25},{17,1},{25,9},{2,18},{10... | collective-permute-start | bytes 122888 | tf_op jit(solution)/shard_map/ppermute | solution.py:417
  27.2 1.6 %collective-permute-done.7.refs_1_ = f32[2,5,8,128]{3,2,1,0:T(8,128)S(1)} collective-permute-done((f32[2,5,8,128]{3,2,1,0:T(8,128)S(1)}, f32[2,5,8,128]{3,2,1,0:T(8,128)S(1)}, u32[]{:S(2)}, u32[]{:S(2)}) %collective-permute-start.7) | collective-permute-done | bytes 40992 | tf_op jit(solution)/shard_map/ppermute | solution.py:417
  28.8 1.3 %collective-permute-done.8.refs_2_ = f32[2,5,8,128]{3,2,1,0:T(8,128)S(1)} collective-permute-done((f32[2,5,8,128]{3,2,1,0:T(8,128)S(1)}, f32[2,5,8,128]{3,2,1,0:T(8,128)S(1)}, u32[]{:S(2)}, u32[]{:S(2)}) %collective-permute-start.8) | collective-permute-done | bytes 40992 | tf_op jit(solution)/shard_map/ppermute | solution.py:417
  30.1 0.5 %collective-permute-done.9.refs_3_ = f32[2,5,8,128]{3,2,1,0:T(8,128)S(1)} collective-permute-done((f32[2,5,8,128]{3,2,1,0:T(8,128)S(1)}, f32[2,5,8,128]{3,2,1,0:T(8,128)S(1)}, u32[]{:S(2)}, u32[]{:S(2)}) %collective-permute-start.9) | collective-permute-done | bytes 40992 | tf_op jit(solution)/shard_map/ppermute | solution.py:417
  30.6 0.7 %unpack.1 = f32[2,5,32,128]{3,2,1,0:T(8,128)} custom-call(f32[2,5,8,128]{3,2,1,0:T(8,128)S(1)} %get-tuple-element.43.refs_0_, f32[2,5,8,128]{3,2,1,0:T(8,128)S(1)} %collective-permute-done.7.refs_1_, f32[2,5,8,128]{3,2,1,0:T(8,128)S(1)} %collective-permute-done.8.refs_2_, f32[2,5,8,128]{3,2,1,0:T(8,128)S(1)} %collective-permute-done.9.refs_3_), custom_call_target="tpu_custom_call" | custom-call | tf_op jit(solution)/shard_map/unpack/pallas_call | solution.py:494
  (5 shorter events, 0.0 us)
Async XLA Ops:
  1.4 8.2 %collective-permute-start.3 = (f32[656,128]{1,0:T(8,128)S(1)}, f32[656,128]{1,0:T(8,128)S(1)}, u32[]{:S(2)}, u32[]{:S(2)}) collective-permute-start(f32[656,128]{1,0:T(8,128)S(1)} %get-tuple-element.30), channel_id=1, source_target_pairs={{0,1},{1,0},{2,3},{3,2},{4,5},{5,4},{6,7},{7,6},{8,9},{9,8},{10,11... | collective-permute-start | bytes 1007624 | tf_op jit(solution)/shard_map/ppermute | solution.py:426
  1.9 7.9 %collective-permute-start = (f32[184,128]{1,0:T(8,128)S(1)}, f32[184,128]{1,0:T(8,128)S(1)}, u32[]{:S(2)}, u32[]{:S(2)}) collective-permute-start(f32[184,128]{1,0:T(8,128)S(1)} %get-tuple-element.27), channel_id=1, source_target_pairs={{0,24},{8,16},{16,8},{24,0},{1,25},{9,17},{17,9},{25,1},{2,26},{10... | collective-permute-start | bytes 282632 | tf_op jit(solution)/shard_map/ppermute | solution.py:417
  5.5 5.6 %collective-permute-start.1 = (f32[184,128]{1,0:T(8,128)S(1)}, f32[184,128]{1,0:T(8,128)S(1)}, u32[]{:S(2)}, u32[]{:S(2)}) collective-permute-start(f32[184,128]{1,0:T(8,128)S(1)} %get-tuple-element.28), channel_id=1, source_target_pairs={{0,8},{8,0},{16,24},{24,16},{1,9},{9,1},{17,25},{25,17},{2,10},{10... | collective-permute-start | bytes 282632 | tf_op jit(solution)/shard_map/ppermute | solution.py:417
  6.0 5.1 %collective-permute-start.2 = (f32[184,128]{1,0:T(8,128)S(1)}, f32[184,128]{1,0:T(8,128)S(1)}, u32[]{:S(2)}, u32[]{:S(2)}) collective-permute-start(f32[184,128]{1,0:T(8,128)S(1)} %get-tuple-element.29), channel_id=1, source_target_pairs={{0,16},{8,24},{16,0},{24,8},{1,17},{9,25},{17,1},{25,9},{2,18},{10... | collective-permute-start | bytes 282632 | tf_op jit(solution)/shard_map/ppermute | solution.py:417
  6.1 11.4 %collective-permute-start.4 = (f32[656,128]{1,0:T(8,128)S(1)}, f32[656,128]{1,0:T(8,128)S(1)}, u32[]{:S(2)}, u32[]{:S(2)}) collective-permute-start(f32[656,128]{1,0:T(8,128)S(1)} %get-tuple-element.40), channel_id=1, source_target_pairs={{1,2},{2,1},{3,4},{4,3},{5,6},{6,5},{0,8},{7,15},{9,10},{10,9},{11... | collective-permute-start | bytes 1007624 | tf_op jit(solution)/shard_map/ppermute | solution.py:425
  11.1 1.6 %collective-permute-start.6 = (f32[552,128]{1,0:T(8,128)S(1)}, f32[552,128]{1,0:T(8,128)S(1)}, u32[]{:S(2)}, u32[]{:S(2)}) collective-permute-start(f32[552,128]{1,0:T(8,128)S(1)} %constant_dynamic-update-slice_fusion), channel_id=1, source_target_pairs={{0,1},{1,0},{2,3},{3,2},{4,5},{5,4},{6,7},{7,6},{8,9},{9,8},{10,11... | collective-permute-start | bytes 847880 | tf_op jit(solution)/shard_map/ppermute | solution.py:462
  11.2 6.7 %collective-permute-start.5 = (f32[552,128]{1,0:T(8,128)S(1)}, f32[552,128]{1,0:T(8,128)S(1)}, u32[]{:S(2)}, u32[]{:S(2)}) collective-permute-start(f32[552,128]{1,0:T(8,128)S(1)} %constant_dynamic-update-slice_fusion), channel_id=1, source_target_pairs={{1,2},{2,1},{3,4},{4,3},{5,6},{6,5},{0,8},{7,15},{9,10},{10,9},{11... | collective-permute-start | bytes 847880 | tf_op jit(solution)/shard_map/ppermute | solution.py:461
  23.6 5.1 %collective-permute-start.7 = (f32[2,5,8,128]{3,2,1,0:T(8,128)S(1)}, f32[2,5,8,128]{3,2,1,0:T(8,128)S(1)}, u32[]{:S(2)}, u32[]{:S(2)}) collective-permute-start(f32[2,5,8,128]{3,2,1,0:T(8,128)S(1)} %get-tuple-element.44), channel_id=1, source_target_pairs={{0,24},{8,16},{16,8},{24,0},{1,25},{9,17},{17,9},{25,1},{2,26},{10... | collective-permute-start | bytes 122888 | tf_op jit(solution)/shard_map/ppermute | solution.py:417
  26.1 4.0 %collective-permute-start.8 = (f32[2,5,8,128]{3,2,1,0:T(8,128)S(1)}, f32[2,5,8,128]{3,2,1,0:T(8,128)S(1)}, u32[]{:S(2)}, u32[]{:S(2)}) collective-permute-start(f32[2,5,8,128]{3,2,1,0:T(8,128)S(1)} %get-tuple-element.45), channel_id=1, source_target_pairs={{0,8},{8,0},{16,24},{24,16},{1,9},{9,1},{17,25},{25,17},{2,10},{10... | collective-permute-start | bytes 122888 | tf_op jit(solution)/shard_map/ppermute | solution.py:417
  26.6 4.0 %collective-permute-start.9 = (f32[2,5,8,128]{3,2,1,0:T(8,128)S(1)}, f32[2,5,8,128]{3,2,1,0:T(8,128)S(1)}, u32[]{:S(2)}, u32[]{:S(2)}) collective-permute-start(f32[2,5,8,128]{3,2,1,0:T(8,128)S(1)} %get-tuple-element.46), channel_id=1, source_target_pairs={{0,16},{8,24},{16,0},{24,8},{1,17},{9,25},{17,1},{25,9},{2,18},{10... | collective-permute-start | bytes 122888 | tf_op jit(solution)/shard_map/ppermute | solution.py:417

commit v3 on v2

--- a/solution.py
+++ b/solution.py
@@ -9,8 +9,10 @@
 
 SWEEPS = 6
 DEEP = SWEEPS - 1
-PARTS = (range(0, 2), range(2, 4), range(4, 7))
-BATCH = PARTS[-1][-1] + 1
+FULL = ((0, range(0, 2)), (1, range(2, 4)), (2, range(4, 7)))
+SHORT = ((0, range(0, 2)), (2, range(2, 5)))
+PARTS = [fields for _, fields in FULL]
+BATCH, REST = FULL[-1][1][-1] + 1, SHORT[-1][1][-1] + 1
 LANES = 128
 TOP = 7
 TALL = 32
@@ -55,22 +57,14 @@
     odd = lax.rem(lax.axis_index("dom"), 2)
     zeros = jnp.zeros((8, LANES), jnp.float32)
     end = 8 + sz.height
-    for copy in copies:
-        copy.wait()
+    for p in range(sz.planes):
+        for pad in [orb_pad.at[j] for j in range(sz.mine)] + [met_pad.at[c] for c in range(7)]:
+            pad[p, 0:8] = zeros
+            pad[p, end : end + 8] = zeros
+    copies[0].wait()
     for p in range(sz.planes):
         for j in range(sz.mine):
-            orb_pad[j, p, 0:8] = zeros
-            orb_pad[j, p, end : end + 8] = zeros
             orb_pad[j, p, 8:end] = orb_ref[j, p]
-        diag = screen_ref[p] + 2.0 * (face_ref[0, p] + face_ref[1, p] + face_ref[2, p])
-        diag = diag + (jnp.abs(cross_ref[0, p]) + jnp.abs(cross_ref[1, p]) + jnp.abs(cross_ref[2, p]))
-        met_pad[6, p, 8:end] = 1.0 / diag
-        for c in range(3):
-            met_pad[c, p, 8:end] = face_ref[c, p]
-            met_pad[3 + c, p, 8:end] = 0.25 * cross_ref[c, p]
-        for c in range(7):
-            met_pad[c, p, 0:8] = zeros
-            met_pad[c, p, end : end + 8] = zeros
     own = 8 + group * sz.rows - DEEP
     for i, s in enumerate(sz.routes):
         first = 8 + jnp.bitwise_xor(group, s) * sz.rows - DEEP
@@ -78,6 +72,15 @@
             for p in range(sz.planes):
                 at = (j * sz.planes + p) * sz.window
                 pieces[i][at : at + sz.window] = orb_pad[j, p, pl.ds(first, sz.window)]
+    for copy in copies[1:]:
+        copy.wait()
+    for p in range(sz.planes):
+        diag = screen_ref[p] + 2.0 * (face_ref[0, p] + face_ref[1, p] + face_ref[2, p])
+        diag = diag + (jnp.abs(cross_ref[0, p]) + jnp.abs(cross_ref[1, p]) + jnp.abs(cross_ref[2, p]))
+        met_pad[6, p, 8:end] = 1.0 / diag
+        for c in range(3):
+            met_pad[c, p, 8:end] = face_ref[c, p]
+            met_pad[3 + c, p, 8:end] = 0.25 * cross_ref[c, p]
     for ref, from_end in ((far_ref, odd), (near_ref, 1 - odd)):
         first_inv = from_end * (sz.planes - DEEP)
         first_met = from_end * (sz.planes - sz.edge)
@@ -116,7 +119,7 @@
     count = jnp.int32(0)
 
     def write(count, first, second, weight):
-        at = 1 + 3 * count
+        at = 2 + 3 * count
         list_ref[at] = first
         list_ref[at + 1] = second
         list_ref[at + 2] = weight
@@ -133,7 +136,9 @@
         seen_ref[k] = 1
     for i in range(BATCH):
         write(count + i, 0, 0, 0)
-    list_ref[0] = (count + BATCH - 1) // BATCH
+    full = (count + BATCH - 1 - REST) // BATCH
+    list_ref[0] = full
+    list_ref[1] = jnp.where(full * BATCH < count, 1, 0)
 
 
 def mirrored(odd, p, count):
@@ -264,14 +269,14 @@
     fill_own(sz, odd, gathered, orbs)
     fill_side(sz, odd, sz.planes + DEEP, near_ref, near_rest, orbs)
 
-    def batch(index, carry):
-        base = index * BATCH
-        firsts = [list_ref[1 + 3 * (base + f)] for f in range(BATCH)]
-        seconds = [list_ref[2 + 3 * (base + f)] for f in range(BATCH)]
-        for fields, start in zip(PARTS, starts):
-            fill_start(sz, orbs, inv, start, fields, firsts, seconds, range(DEEP, sz.span))
+    def batch(parts, base, carry):
+        size = parts[-1][1][-1] + 1
+        firsts = [list_ref[2 + 3 * (base + f)] for f in range(size)]
+        seconds = [list_ref[3 + 3 * (base + f)] for f in range(size)]
+        for h, fields in parts:
+            fill_start(sz, orbs, inv, starts[h], fields, firsts, seconds, range(DEEP, sz.span))
         for number in range(1, DEEP):
-            for h, fields in enumerate(PARTS):
+            for h, fields in parts:
                 start, low = starts[h], fields[0]
                 source = start if number == 1 else levels[h * (DEEP - 2) + number - 2]
                 planes = list(range(DEEP + number, sz.span - number))
@@ -289,7 +294,9 @@
                     sweep(load, start, coef, fields, row, planes, put)
         return carry
 
-    lax.fori_loop(0, list_ref[0], batch, 0)
+    full = list_ref[0]
+    lax.fori_loop(0, full, lambda i, carry: batch(FULL, i * BATCH, carry), 0)
+    lax.fori_loop(0, list_ref[1], lambda i, carry: batch(SHORT, full * BATCH, carry), 0)
 
 
 def far_kernel(sz, slabs, list_ref, *refs):
@@ -316,20 +323,20 @@
         for p in range(n):
             total[i, p] = jnp.zeros((8, LANES), jnp.float32)
 
-    def batch(index, carry):
-        base = index * BATCH
-        firsts = [list_ref[1 + 3 * (base + f)] for f in range(BATCH)]
-        seconds = [list_ref[2 + 3 * (base + f)] for f in range(BATCH)]
+    def batch(parts, base, carry):
+        size = parts[-1][1][-1] + 1
+        firsts = [list_ref[2 + 3 * (base + f)] for f in range(size)]
+        seconds = [list_ref[3 + 3 * (base + f)] for f in range(size)]
         weights = []
-        for f in range(BATCH):
-            w = list_ref[3 + 3 * (base + f)]
+        for f in range(size):
+            w = list_ref[4 + 3 * (base + f)]
             weights.append(
                 (w.astype(jnp.float32), jnp.where(firsts[f] == seconds[f], 0, w).astype(jnp.float32))
             )
-        for fields, start in zip(PARTS, starts):
-            fill_start(sz, orbs, inv, start, fields, firsts, seconds, range(DEEP + n))
+        for h, fields in parts:
+            fill_start(sz, orbs, inv, starts[h], fields, firsts, seconds, range(DEEP + n))
         for number in range(1, DEEP + 1):
-            for h, fields in enumerate(PARTS):
+            for h, fields in parts:
                 start, low = starts[h], fields[0]
                 planes = list(range(number, number + n))
 
@@ -359,7 +366,9 @@
                     sweep(load, start, coef, fields, row, planes, put)
         return carry
 
-    lax.fori_loop(0, list_ref[0], batch, 0)
+    full = list_ref[0]
+    lax.fori_loop(0, full, lambda i, carry: batch(FULL, i * BATCH, carry), 0)
+    lax.fori_loop(0, list_ref[1], lambda i, carry: batch(SHORT, full * BATCH, carry), 0)
 
     for i, s in enumerate(sz.routes):
         for j in range(sz.mine):
@@ -432,7 +441,7 @@
     points = sz.rows * planes * lanes
     pairs = pl.pallas_call(
         functools.partial(list_kernel, sz),
-        out_shape=jax.ShapeDtypeStruct((1 + 3 * room,), jnp.int32),
+        out_shape=jax.ShapeDtypeStruct((2 + 3 * room,), jnp.int32),
         in_specs=[hbm],
         out_specs=smem,
         scratch_shapes=[

time: 31.4 us -> 31.2 us (level)
  Pallas kernels: 14.5 us -> 13.6 us
  waiting for transfers between devices: 4.92 us -> 5.33 us
    pallas_call x1, Pallas kernels: 5.79 us -> 5.36 us  [body(): pl.pallas_call(functools.partial(far_kernel, sz, slabs), out_shape=[jax.S...]
    ppermute x1, waiting for transfers between devices: 0.32 us -> 0.72 us  [body(): far_rest = lax.ppermute(rest, ('orb', 'dom'), to_far)]
    pallas_call x1, Pallas kernels: 4.76 us -> 4.37 us  [body(): pl.pallas_call(functools.partial(near_kernel, sz), out_shape=jax.ShapeDty...]
  transfers between devices with their start and end apart: 10 -> 10, of which waited for: 5 -> 5; matrix products, arithmetic and copies ran while one was open for 0% -> 0% of each run, Pallas kernels for 21% -> 20%
where the time goes in v3:
time: 31.2 us; the launch traced here: 30.8 us
  Pallas kernels  13.6 us (44%)
  starting transfers between devices  11.8 us (38%)
  waiting for transfers between devices  5.33 us (17%)
    ppermute x6, starting transfers between devices, swap(): return lax.ppermute(x, 'orb', [(i, i ^ s) for i in range(groups)])  7.72 us
    pallas_call x1, Pallas kernels, body(): pl.pallas_call(functools.partial(far_kernel, sz, slabs), out_shape=[jax.S...  5.36 us
    ppermute x6, waiting for transfers between devices, swap(): return lax.ppermute(x, 'orb', [(i, i ^ s) for i in range(groups)])  4.6 us
    pallas_call x1, Pallas kernels, body(): pl.pallas_call(functools.partial(near_kernel, sz), out_shape=jax.ShapeDty...  4.37 us
    ppermute x1, starting transfers between devices, body(): far_side = lax.ppermute(far, ('orb', 'dom'), to_far)  1.89 us
    pallas_call x1, Pallas kernels, body(): pl.pallas_call(functools.partial(list_kernel, sz), out_shape=jax.ShapeDty...  1.59 us
    ppermute x1, starting transfers between devices, body(): far_rest = lax.ppermute(rest, ('orb', 'dom'), to_far)  1.56 us
    pallas_call x1, Pallas kernels, body(): pl.pallas_call(functools.partial(pack_kernel, sz), out_shape=[jax.ShapeDt...  1.36 us
  transfers between devices with their start and end apart: 10, of which 5 were waited for; matrix products, arithmetic and copies ran while one was open for 0% of the time, Pallas kernels for 20%

profile of v3, /device:TPU:0, one launch (start us, length us, event | category | flops | bytes accessed | tf_op | source)
XLA Modules:
  0.0 30.8 jit_solution(15172247354804505408)
XLA Ops:
  0.0 1.4 %pack.1 = (f32[184,128]{1,0:T(8,128)S(1)}, f32[184,128]{1,0:T(8,128)S(1)}, f32[184,128]{1,0:T(8,128)S(1)}, f32[184,128]{1,0:T(8,128)S(1)}, f32[656,128]{1,0:T(8,...) custom-call(f32[2,5,32,128]{3,2,1,0:T(8,128)} %orb_in.1, ...), custom_call_target="tpu_custom_call" | custom-call | tf_op jit(solution)/shard_map/pack/pallas_call | solution.py:400
  1.4 0.5 %collective-permute-start.3 = (f32[656,128]{1,0:T(8,128)S(1)}, f32[656,128]{1,0:T(8,128)S(1)}, u32[]{:S(2)}, u32[]{:S(2)}) collective-permute-start(f32[656,128]{1,0:T(8,128)S(1)} %get-tuple-element.30), channel_id=1, source_target_pairs={{0,1},{1,0},{2,3},{3,2},{4,5},{5,4},{6,7},{7,6},{8,9},{9,8},{10,11... | collective-permute-start | bytes 1007624 | tf_op jit(solution)/shard_map/ppermute | solution.py:435
  1.9 3.5 %collective-permute-start = (f32[184,128]{1,0:T(8,128)S(1)}, f32[184,128]{1,0:T(8,128)S(1)}, u32[]{:S(2)}, u32[]{:S(2)}) collective-permute-start(f32[184,128]{1,0:T(8,128)S(1)} %get-tuple-element.27), channel_id=1, source_target_pairs={{0,24},{8,16},{16,8},{24,0},{1,25},{9,17},{17,9},{25,1},{2,26},{10... | collective-permute-start | bytes 282632 | tf_op jit(solution)/shard_map/ppermute | solution.py:426
  5.4 0.5 %collective-permute-start.1 = (f32[184,128]{1,0:T(8,128)S(1)}, f32[184,128]{1,0:T(8,128)S(1)}, u32[]{:S(2)}, u32[]{:S(2)}) collective-permute-start(f32[184,128]{1,0:T(8,128)S(1)} %get-tuple-element.28), channel_id=1, source_target_pairs={{0,8},{8,0},{16,24},{24,16},{1,9},{9,1},{17,25},{25,17},{2,10},{10... | collective-permute-start | bytes 282632 | tf_op jit(solution)/shard_map/ppermute | solution.py:426
  5.9 0.1 collective-permute-start.2
  6.0 1.9 %collective-permute-start.4 = (f32[656,128]{1,0:T(8,128)S(1)}, f32[656,128]{1,0:T(8,128)S(1)}, u32[]{:S(2)}, u32[]{:S(2)}) collective-permute-start(f32[656,128]{1,0:T(8,128)S(1)} %get-tuple-element.40), channel_id=1, source_target_pairs={{1,2},{2,1},{3,4},{4,3},{5,6},{6,5},{0,8},{7,15},{9,10},{10,9},{11... | collective-permute-start | bytes 1007624 | tf_op jit(solution)/shard_map/ppermute | solution.py:434
  7.9 1.6 %pairs.1.list_ref = s32[119]{0:T(128)S(1)} custom-call(s32[4]{0:T(128)} %turn_in.1), custom_call_target="tpu_custom_call" | custom-call | tf_op jit(solution)/shard_map/pairs/pallas_call | solution.py:442
  9.5 0.0 collective-permute-done.3.near_ref.refs_4_
  9.6 0.3 coefs.1
  9.8 0.0 collective-permute-done.refs_1_
  9.8 1.2 %collective-permute-done.1.refs_2_ = f32[184,128]{1,0:T(8,128)S(1)} collective-permute-done((f32[184,128]{1,0:T(8,128)S(1)}, f32[184,128]{1,0:T(8,128)S(1)}, u32[]{:S(2)}, u32[]{:S(2)}) %collective-permute-start.1) | collective-permute-done | bytes 94240 | tf_op jit(solution)/shard_map/ppermute | solution.py:426
  11.0 0.0 collective-permute-done.2.refs_3_
  11.0 0.1 collective-permute-start.6
  11.1 1.6 %collective-permute-start.5 = (f32[552,128]{1,0:T(8,128)S(1)}, f32[552,128]{1,0:T(8,128)S(1)}, u32[]{:S(2)}, u32[]{:S(2)}) collective-permute-start(f32[552,128]{1,0:T(8,128)S(1)} %constant_dynamic-update-slice_fusion), channel_id=1, source_target_pairs={{1,2},{2,1},{3,4},{4,3},{5,6},{6,5},{0,8},{7,15},{9,10},{10,9},{11... | collective-permute-start | bytes 847880 | tf_op jit(solution)/shard_map/ppermute | solution.py:470
  12.7 4.4 %near.1.refs_8_ = f32[28,4,2,32,128]{4,3,2,1,0:T(8,128)S(1)} custom-call(s32[119]{0:T(128)S(1)} %pairs.1.list_ref, f32[184,128]{1,0:T(8,128)S(1)} %get-tuple-element.36.refs_0_, f32[184,128]{1,0:T(8,128)S(1)} %collective-permute-done.refs_1_, f32[184,128]{1,0:T(8,128)S(1)} %collective-permute-done.1.refs_2_, f32[184,128]{1,0:T(8,128)S(1)} %collective-permute-done.2.refs_3_, ...), custom_call_target="tpu_custom_call" | custom-call | flops 28672000 | bytes 20000000 | tf_op jit(solution)/shard_map/near/pallas_call | solution.py:475
  17.1 0.7 %collective-permute-done.5.refs_5_ = f32[552,128]{1,0:T(8,128)S(1)} collective-permute-done((f32[552,128]{1,0:T(8,128)S(1)}, f32[552,128]{1,0:T(8,128)S(1)}, u32[]{:S(2)}, u32[]{:S(2)}) %collective-permute-start.5) | collective-permute-done | bytes 282656 | tf_op jit(solution)/shard_map/ppermute | solution.py:470
  17.8 5.4 %far.1 = (f32[2,5,8,128]{3,2,1,0:T(8,128)S(1)}, f32[2,5,8,128]{3,2,1,0:T(8,128)S(1)}, f32[2,5,8,128]{3,2,1,0:T(8,128)S(1)}, f32[2,5,8,128]{3,2,1,0:T(8,128)S(1)}) custom-call(s32[119]{0:T(128)S(1)} %pairs.1.list_ref, f32[184,128]{1,0:T(8,128)S(1)} %get-tuple-element.36.refs_0_, f32[184,128]{1,0:T(8,128)S(1)} %collective-permute-done.refs_1_, ...), custom_call_target="tpu_custom_call" | custom-call | tf_op jit(solution)/shard_map/far/pallas_call | solution.py:485
  23.1 2.5 %collective-permute-start.7 = (f32[2,5,8,128]{3,2,1,0:T(8,128)S(1)}, f32[2,5,8,128]{3,2,1,0:T(8,128)S(1)}, u32[]{:S(2)}, u32[]{:S(2)}) collective-permute-start(f32[2,5,8,128]{3,2,1,0:T(8,128)S(1)} %get-tuple-element.44), channel_id=1, source_target_pairs={{0,24},{8,16},{16,8},{24,0},{1,25},{9,17},{17,9},{25,1},{2,26},{10... | collective-permute-start | bytes 122888 | tf_op jit(solution)/shard_map/ppermute | solution.py:426
  25.6 0.5 %collective-permute-start.8 = (f32[2,5,8,128]{3,2,1,0:T(8,128)S(1)}, f32[2,5,8,128]{3,2,1,0:T(8,128)S(1)}, u32[]{:S(2)}, u32[]{:S(2)}) collective-permute-start(f32[2,5,8,128]{3,2,1,0:T(8,128)S(1)} %get-tuple-element.45), channel_id=1, source_target_pairs={{0,8},{8,0},{16,24},{24,16},{1,9},{9,1},{17,25},{25,17},{2,10},{10... | collective-permute-start | bytes 122888 | tf_op jit(solution)/shard_map/ppermute | solution.py:426
  26.1 0.6 %collective-permute-start.9 = (f32[2,5,8,128]{3,2,1,0:T(8,128)S(1)}, f32[2,5,8,128]{3,2,1,0:T(8,128)S(1)}, u32[]{:S(2)}, u32[]{:S(2)}) collective-permute-start(f32[2,5,8,128]{3,2,1,0:T(8,128)S(1)} %get-tuple-element.46), channel_id=1, source_target_pairs={{0,16},{8,24},{16,0},{24,8},{1,17},{9,25},{17,1},{25,9},{2,18},{10... | collective-permute-start | bytes 122888 | tf_op jit(solution)/shard_map/ppermute | solution.py:426
  26.7 1.6 %collective-permute-done.7.refs_1_ = f32[2,5,8,128]{3,2,1,0:T(8,128)S(1)} collective-permute-done((f32[2,5,8,128]{3,2,1,0:T(8,128)S(1)}, f32[2,5,8,128]{3,2,1,0:T(8,128)S(1)}, u32[]{:S(2)}, u32[]{:S(2)}) %collective-permute-start.7) | collective-permute-done | bytes 40992 | tf_op jit(solution)/shard_map/ppermute | solution.py:426
  28.3 1.3 %collective-permute-done.8.refs_2_ = f32[2,5,8,128]{3,2,1,0:T(8,128)S(1)} collective-permute-done((f32[2,5,8,128]{3,2,1,0:T(8,128)S(1)}, f32[2,5,8,128]{3,2,1,0:T(8,128)S(1)}, u32[]{:S(2)}, u32[]{:S(2)}) %collective-permute-start.8) | collective-permute-done | bytes 40992 | tf_op jit(solution)/shard_map/ppermute | solution.py:426
  29.6 0.5 %collective-permute-done.9.refs_3_ = f32[2,5,8,128]{3,2,1,0:T(8,128)S(1)} collective-permute-done((f32[2,5,8,128]{3,2,1,0:T(8,128)S(1)}, f32[2,5,8,128]{3,2,1,0:T(8,128)S(1)}, u32[]{:S(2)}, u32[]{:S(2)}) %collective-permute-start.9) | collective-permute-done | bytes 40992 | tf_op jit(solution)/shard_map/ppermute | solution.py:426
  30.1 0.7 %unpack.1 = f32[2,5,32,128]{3,2,1,0:T(8,128)} custom-call(f32[2,5,8,128]{3,2,1,0:T(8,128)S(1)} %get-tuple-element.43.refs_0_, f32[2,5,8,128]{3,2,1,0:T(8,128)S(1)} %collective-permute-done.7.refs_1_, f32[2,5,8,128]{3,2,1,0:T(8,128)S(1)} %collective-permute-done.8.refs_2_, f32[2,5,8,128]{3,2,1,0:T(8,128)S(1)} %collective-permute-done.9.refs_3_), custom_call_target="tpu_custom_call" | custom-call | tf_op jit(solution)/shard_map/unpack/pallas_call | solution.py:503
  (5 shorter events, 0.0 us)
Async XLA Ops:
  1.4 8.2 %collective-permute-start.3 = (f32[656,128]{1,0:T(8,128)S(1)}, f32[656,128]{1,0:T(8,128)S(1)}, u32[]{:S(2)}, u32[]{:S(2)}) collective-permute-start(f32[656,128]{1,0:T(8,128)S(1)} %get-tuple-element.30), channel_id=1, source_target_pairs={{0,1},{1,0},{2,3},{3,2},{4,5},{5,4},{6,7},{7,6},{8,9},{9,8},{10,11... | collective-permute-start | bytes 1007624 | tf_op jit(solution)/shard_map/ppermute | solution.py:435
  1.9 7.9 %collective-permute-start = (f32[184,128]{1,0:T(8,128)S(1)}, f32[184,128]{1,0:T(8,128)S(1)}, u32[]{:S(2)}, u32[]{:S(2)}) collective-permute-start(f32[184,128]{1,0:T(8,128)S(1)} %get-tuple-element.27), channel_id=1, source_target_pairs={{0,24},{8,16},{16,8},{24,0},{1,25},{9,17},{17,9},{25,1},{2,26},{10... | collective-permute-start | bytes 282632 | tf_op jit(solution)/shard_map/ppermute | solution.py:426
  5.4 5.6 %collective-permute-start.1 = (f32[184,128]{1,0:T(8,128)S(1)}, f32[184,128]{1,0:T(8,128)S(1)}, u32[]{:S(2)}, u32[]{:S(2)}) collective-permute-start(f32[184,128]{1,0:T(8,128)S(1)} %get-tuple-element.28), channel_id=1, source_target_pairs={{0,8},{8,0},{16,24},{24,16},{1,9},{9,1},{17,25},{25,17},{2,10},{10... | collective-permute-start | bytes 282632 | tf_op jit(solution)/shard_map/ppermute | solution.py:426
  5.9 5.1 %collective-permute-start.2 = (f32[184,128]{1,0:T(8,128)S(1)}, f32[184,128]{1,0:T(8,128)S(1)}, u32[]{:S(2)}, u32[]{:S(2)}) collective-permute-start(f32[184,128]{1,0:T(8,128)S(1)} %get-tuple-element.29), channel_id=1, source_target_pairs={{0,16},{8,24},{16,0},{24,8},{1,17},{9,25},{17,1},{25,9},{2,18},{10... | collective-permute-start | bytes 282632 | tf_op jit(solution)/shard_map/ppermute | solution.py:426
  6.0 11.0 %collective-permute-start.4 = (f32[656,128]{1,0:T(8,128)S(1)}, f32[656,128]{1,0:T(8,128)S(1)}, u32[]{:S(2)}, u32[]{:S(2)}) collective-permute-start(f32[656,128]{1,0:T(8,128)S(1)} %get-tuple-element.40), channel_id=1, source_target_pairs={{1,2},{2,1},{3,4},{4,3},{5,6},{6,5},{0,8},{7,15},{9,10},{10,9},{11... | collective-permute-start | bytes 1007624 | tf_op jit(solution)/shard_map/ppermute | solution.py:434
  11.0 1.6 %collective-permute-start.6 = (f32[552,128]{1,0:T(8,128)S(1)}, f32[552,128]{1,0:T(8,128)S(1)}, u32[]{:S(2)}, u32[]{:S(2)}) collective-permute-start(f32[552,128]{1,0:T(8,128)S(1)} %constant_dynamic-update-slice_fusion), channel_id=1, source_target_pairs={{0,1},{1,0},{2,3},{3,2},{4,5},{5,4},{6,7},{7,6},{8,9},{9,8},{10,11... | collective-permute-start | bytes 847880 | tf_op jit(solution)/shard_map/ppermute | solution.py:471
  11.1 6.7 %collective-permute-start.5 = (f32[552,128]{1,0:T(8,128)S(1)}, f32[552,128]{1,0:T(8,128)S(1)}, u32[]{:S(2)}, u32[]{:S(2)}) collective-permute-start(f32[552,128]{1,0:T(8,128)S(1)} %constant_dynamic-update-slice_fusion), channel_id=1, source_target_pairs={{1,2},{2,1},{3,4},{4,3},{5,6},{6,5},{0,8},{7,15},{9,10},{10,9},{11... | collective-permute-start | bytes 847880 | tf_op jit(solution)/shard_map/ppermute | solution.py:470
  23.1 5.1 %collective-permute-start.7 = (f32[2,5,8,128]{3,2,1,0:T(8,128)S(1)}, f32[2,5,8,128]{3,2,1,0:T(8,128)S(1)}, u32[]{:S(2)}, u32[]{:S(2)}) collective-permute-start(f32[2,5,8,128]{3,2,1,0:T(8,128)S(1)} %get-tuple-element.44), channel_id=1, source_target_pairs={{0,24},{8,16},{16,8},{24,0},{1,25},{9,17},{17,9},{25,1},{2,26},{10... | collective-permute-start | bytes 122888 | tf_op jit(solution)/shard_map/ppermute | solution.py:426
  25.6 4.0 %collective-permute-start.8 = (f32[2,5,8,128]{3,2,1,0:T(8,128)S(1)}, f32[2,5,8,128]{3,2,1,0:T(8,128)S(1)}, u32[]{:S(2)}, u32[]{:S(2)}) collective-permute-start(f32[2,5,8,128]{3,2,1,0:T(8,128)S(1)} %get-tuple-element.45), channel_id=1, source_target_pairs={{0,8},{8,0},{16,24},{24,16},{1,9},{9,1},{17,25},{25,17},{2,10},{10... | collective-permute-start | bytes 122888 | tf_op jit(solution)/shard_map/ppermute | solution.py:426
  26.1 4.0 %collective-permute-start.9 = (f32[2,5,8,128]{3,2,1,0:T(8,128)S(1)}, f32[2,5,8,128]{3,2,1,0:T(8,128)S(1)}, u32[]{:S(2)}, u32[]{:S(2)}) collective-permute-start(f32[2,5,8,128]{3,2,1,0:T(8,128)S(1)} %get-tuple-element.46), channel_id=1, source_target_pairs={{0,16},{8,24},{16,0},{24,8},{1,17},{9,25},{17,1},{25,9},{2,18},{10... | collective-permute-start | bytes 122888 | tf_op jit(solution)/shard_map/ppermute | solution.py:426

commit v4 on v3

--- a/solution.py
+++ b/solution.py
@@ -303,7 +303,8 @@
     gathered = refs[: sz.groups]
     far_ref, far_rest, inv, coef, state = refs[sz.groups : sz.groups + 5]
     outs = refs[sz.groups + 5 : 2 * sz.groups + 5]
-    orbs, total, inv_far, coef_far, *refs = refs[2 * sz.groups + 5 :]
+    orbs, inv_far, coef_far, *refs = refs[2 * sz.groups + 5 :]
+    totals, refs = refs[:BATCH], refs[BATCH:]
     starts, refs = refs[: len(PARTS)], refs[len(PARTS) :]
     every = len(PARTS) * (DEEP - 1)
     levels = refs[:every]
@@ -321,7 +322,8 @@
     fill_side(sz, odd, 0, far_ref, far_rest, orbs)
     for i in range(sz.orbs):
         for p in range(n):
-            total[i, p] = jnp.zeros((8, LANES), jnp.float32)
+            for total in totals:
+                total[i, p] = jnp.zeros((8, LANES), jnp.float32)
 
     def batch(parts, base, carry):
         size = parts[-1][1][-1] + 1
@@ -360,6 +362,7 @@
                     def put(f, p, new, row=row):
                         a, b = firsts[f], seconds[f]
                         q = p - DEEP
+                        total = totals[f]
                         total[a, q] = total[a, q] + (weights[f][0] * new) * orbs[b, p, row : row + 8]
                         total[b, q] = total[b, q] + (weights[f][1] * new) * orbs[a, p, row : row + 8]
 
@@ -373,7 +376,8 @@
     for i, s in enumerate(sz.routes):
         for j in range(sz.mine):
             for p in range(n):
-                outs[i][j, p] = total[s * sz.mine + j, mirrored(odd, p, n), 0 : sz.rows]
+                at = mirrored(odd, p, n)
+                outs[i][j, p] = sum(total[s * sz.mine + j, at, 0 : sz.rows] for total in totals)
 
 
 def unpack_kernel(sz, *refs):
@@ -489,10 +493,10 @@
         out_specs=[vmem] * groups,
         scratch_shapes=[
             orbital_windows,
-            pltpu.VMEM((sz.orbs, planes, 8, lanes), f32),
             pltpu.VMEM((DEEP, TALL, lanes), f32),
             pltpu.VMEM((9, DEEP, 16, lanes), f32),
         ]
+        + [pltpu.VMEM((sz.orbs, planes, 8, lanes), f32)] * BATCH
         + field
         + [x for x in field for _ in range(DEEP - 1)]
        ,

time: 31.2 us -> 32.8 us (1.051)
  Pallas kernels: 13.6 us -> 16.1 us
  waiting for transfers between devices: 5.33 us -> 4.61 us
    pallas_call x1, Pallas kernels: 4.37 us -> 5.74 us  [body(): pl.pallas_call(functools.partial(near_kernel, sz), out_shape=jax.ShapeDty...]
    pallas_call x1, Pallas kernels: 5.36 us -> 6.48 us  [body(): pl.pallas_call(functools.partial(far_kernel, sz, slabs), out_shape=[jax.S...]
    ppermute x1, waiting for transfers between devices: 0.72 us -> 0.01 us  [body(): far_rest = lax.ppermute(rest, ('orb', 'dom'), to_far)]
  transfers between devices with their start and end apart: 10 -> 10, of which waited for: 5 -> 4; matrix products, arithmetic and copies ran while one was open for 0% -> 0% of each run, Pallas kernels for 20% -> 23%
where the time goes in v4:
time: 32.8 us; the launch traced here: 32.6 us
  Pallas kernels  16.1 us (49%)
  starting transfers between devices  11.8 us (36%)
  waiting for transfers between devices  4.61 us (14%)
    ppermute x6, starting transfers between devices, swap(): return lax.ppermute(x, 'orb', [(i, i ^ s) for i in range(groups)])  7.72 us
    pallas_call x1, Pallas kernels, body(): pl.pallas_call(functools.partial(far_kernel, sz, slabs), out_shape=[jax.S...  6.48 us
    pallas_call x1, Pallas kernels, body(): pl.pallas_call(functools.partial(near_kernel, sz), out_shape=jax.ShapeDty...  5.74 us
    ppermute x6, waiting for transfers between devices, swap(): return lax.ppermute(x, 'orb', [(i, i ^ s) for i in range(groups)])  4.6 us
    ppermute x1, starting transfers between devices, body(): far_side = lax.ppermute(far, ('orb', 'dom'), to_far)  1.89 us
    pallas_call x1, Pallas kernels, body(): pl.pallas_call(functools.partial(list_kernel, sz), out_shape=jax.ShapeDty...  1.59 us
    ppermute x1, starting transfers between devices, body(): far_rest = lax.ppermute(rest, ('orb', 'dom'), to_far)  1.56 us
    pallas_call x1, Pallas kernels, body(): pl.pallas_call(functools.partial(pack_kernel, sz), out_shape=[jax.ShapeDt...  1.36 us
  transfers between devices with their start and end apart: 10, of which 4 were waited for; matrix products, arithmetic and copies ran while one was open for 0% of the time, Pallas kernels for 23%

profile of v4, /device:TPU:0, one launch (start us, length us, event | category | flops | bytes accessed | tf_op | source)
XLA Modules:
  0.0 32.6 jit_solution(18440631028379392253)
XLA Ops:
  0.0 1.4 %pack.1 = (f32[184,128]{1,0:T(8,128)S(1)}, f32[184,128]{1,0:T(8,128)S(1)}, f32[184,128]{1,0:T(8,128)S(1)}, f32[184,128]{1,0:T(8,128)S(1)}, f32[656,128]{1,0:T(8,...) custom-call(f32[2,5,32,128]{3,2,1,0:T(8,128)} %orb_in.1, ...), custom_call_target="tpu_custom_call" | custom-call | tf_op jit(solution)/shard_map/pack/pallas_call | solution.py:404
  1.4 0.5 %collective-permute-start.3 = (f32[656,128]{1,0:T(8,128)S(1)}, f32[656,128]{1,0:T(8,128)S(1)}, u32[]{:S(2)}, u32[]{:S(2)}) collective-permute-start(f32[656,128]{1,0:T(8,128)S(1)} %get-tuple-element.30), channel_id=1, source_target_pairs={{0,1},{1,0},{2,3},{3,2},{4,5},{5,4},{6,7},{7,6},{8,9},{9,8},{10,11... | collective-permute-start | bytes 1007624 | tf_op jit(solution)/shard_map/ppermute | solution.py:439
  1.9 3.5 %collective-permute-start = (f32[184,128]{1,0:T(8,128)S(1)}, f32[184,128]{1,0:T(8,128)S(1)}, u32[]{:S(2)}, u32[]{:S(2)}) collective-permute-start(f32[184,128]{1,0:T(8,128)S(1)} %get-tuple-element.27), channel_id=1, source_target_pairs={{0,24},{8,16},{16,8},{24,0},{1,25},{9,17},{17,9},{25,1},{2,26},{10... | collective-permute-start | bytes 282632 | tf_op jit(solution)/shard_map/ppermute | solution.py:430
  5.4 0.5 %collective-permute-start.1 = (f32[184,128]{1,0:T(8,128)S(1)}, f32[184,128]{1,0:T(8,128)S(1)}, u32[]{:S(2)}, u32[]{:S(2)}) collective-permute-start(f32[184,128]{1,0:T(8,128)S(1)} %get-tuple-element.28), channel_id=1, source_target_pairs={{0,8},{8,0},{16,24},{24,16},{1,9},{9,1},{17,25},{25,17},{2,10},{10... | collective-permute-start | bytes 282632 | tf_op jit(solution)/shard_map/ppermute | solution.py:430
  5.9 0.1 collective-permute-start.2
  6.0 1.9 %collective-permute-start.4 = (f32[656,128]{1,0:T(8,128)S(1)}, f32[656,128]{1,0:T(8,128)S(1)}, u32[]{:S(2)}, u32[]{:S(2)}) collective-permute-start(f32[656,128]{1,0:T(8,128)S(1)} %get-tuple-element.40), channel_id=1, source_target_pairs={{1,2},{2,1},{3,4},{4,3},{5,6},{6,5},{0,8},{7,15},{9,10},{10,9},{11... | collective-permute-start | bytes 1007624 | tf_op jit(solution)/shard_map/ppermute | solution.py:438
  7.9 1.6 %pairs.1.list_ref = s32[119]{0:T(128)S(1)} custom-call(s32[4]{0:T(128)} %turn_in.1), custom_call_target="tpu_custom_call" | custom-call | tf_op jit(solution)/shard_map/pairs/pallas_call | solution.py:446
  9.5 0.0 collective-permute-done.3.near_ref.refs_4_
  9.6 0.3 coefs.1
  9.8 0.0 collective-permute-done.refs_1_
  9.8 1.2 %collective-permute-done.1.refs_2_ = f32[184,128]{1,0:T(8,128)S(1)} collective-permute-done((f32[184,128]{1,0:T(8,128)S(1)}, f32[184,128]{1,0:T(8,128)S(1)}, u32[]{:S(2)}, u32[]{:S(2)}) %collective-permute-start.1) | collective-permute-done | bytes 94240 | tf_op jit(solution)/shard_map/ppermute | solution.py:430
  11.0 0.0 collective-permute-done.2.refs_3_
  11.0 0.1 collective-permute-start.6
  11.1 1.6 %collective-permute-start.5 = (f32[552,128]{1,0:T(8,128)S(1)}, f32[552,128]{1,0:T(8,128)S(1)}, u32[]{:S(2)}, u32[]{:S(2)}) collective-permute-start(f32[552,128]{1,0:T(8,128)S(1)} %constant_dynamic-update-slice_fusion), channel_id=1, source_target_pairs={{1,2},{2,1},{3,4},{4,3},{5,6},{6,5},{0,8},{7,15},{9,10},{10,9},{11... | collective-permute-start | bytes 847880 | tf_op jit(solution)/shard_map/ppermute | solution.py:474
  12.7 5.7 %near.1.refs_8_ = f32[28,4,2,32,128]{4,3,2,1,0:T(8,128)S(1)} custom-call(s32[119]{0:T(128)S(1)} %pairs.1.list_ref, f32[184,128]{1,0:T(8,128)S(1)} %get-tuple-element.36.refs_0_, f32[184,128]{1,0:T(8,128)S(1)} %collective-permute-done.refs_1_, f32[184,128]{1,0:T(8,128)S(1)} %collective-permute-done.1.refs_2_, f32[184,128]{1,0:T(8,128)S(1)} %collective-permute-done.2.refs_3_, ...), custom_call_target="tpu_custom_call" | custom-call | flops 28672000 | bytes 20000000 | tf_op jit(solution)/shard_map/near/pallas_call | solution.py:479
  18.4 0.0 collective-permute-done.4.refs_4_
  18.4 6.5 %far.1 = (f32[2,5,8,128]{3,2,1,0:T(8,128)S(1)}, f32[2,5,8,128]{3,2,1,0:T(8,128)S(1)}, f32[2,5,8,128]{3,2,1,0:T(8,128)S(1)}, f32[2,5,8,128]{3,2,1,0:T(8,128)S(1)}) custom-call(s32[119]{0:T(128)S(1)} %pairs.1.list_ref, f32[184,128]{1,0:T(8,128)S(1)} %get-tuple-element.36.refs_0_, f32[184,128]{1,0:T(8,128)S(1)} %collective-permute-done.refs_1_, ...), custom_call_target="tpu_custom_call" | custom-call | tf_op jit(solution)/shard_map/far/pallas_call | solution.py:489
  24.9 2.4 %collective-permute-start.7 = (f32[2,5,8,128]{3,2,1,0:T(8,128)S(1)}, f32[2,5,8,128]{3,2,1,0:T(8,128)S(1)}, u32[]{:S(2)}, u32[]{:S(2)}) collective-permute-start(f32[2,5,8,128]{3,2,1,0:T(8,128)S(1)} %get-tuple-element.44), channel_id=1, source_target_pairs={{0,24},{8,16},{16,8},{24,0},{1,25},{9,17},{17,9},{25,1},{2,26},{10... | collective-permute-start | bytes 122888 | tf_op jit(solution)/shard_map/ppermute | solution.py:430
  27.4 0.6 %collective-permute-start.8 = (f32[2,5,8,128]{3,2,1,0:T(8,128)S(1)}, f32[2,5,8,128]{3,2,1,0:T(8,128)S(1)}, u32[]{:S(2)}, u32[]{:S(2)}) collective-permute-start(f32[2,5,8,128]{3,2,1,0:T(8,128)S(1)} %get-tuple-element.45), channel_id=1, source_target_pairs={{0,8},{8,0},{16,24},{24,16},{1,9},{9,1},{17,25},{25,17},{2,10},{10... | collective-permute-start | bytes 122888 | tf_op jit(solution)/shard_map/ppermute | solution.py:430
  27.9 0.6 %collective-permute-start.9 = (f32[2,5,8,128]{3,2,1,0:T(8,128)S(1)}, f32[2,5,8,128]{3,2,1,0:T(8,128)S(1)}, u32[]{:S(2)}, u32[]{:S(2)}) collective-permute-start(f32[2,5,8,128]{3,2,1,0:T(8,128)S(1)} %get-tuple-element.46), channel_id=1, source_target_pairs={{0,16},{8,24},{16,0},{24,8},{1,17},{9,25},{17,1},{25,9},{2,18},{10... | collective-permute-start | bytes 122888 | tf_op jit(solution)/shard_map/ppermute | solution.py:430
  28.5 1.4 %collective-permute-done.7.refs_1_ = f32[2,5,8,128]{3,2,1,0:T(8,128)S(1)} collective-permute-done((f32[2,5,8,128]{3,2,1,0:T(8,128)S(1)}, f32[2,5,8,128]{3,2,1,0:T(8,128)S(1)}, u32[]{:S(2)}, u32[]{:S(2)}) %collective-permute-start.7) | collective-permute-done | bytes 40992 | tf_op jit(solution)/shard_map/ppermute | solution.py:430
  29.9 1.5 %collective-permute-done.8.refs_2_ = f32[2,5,8,128]{3,2,1,0:T(8,128)S(1)} collective-permute-done((f32[2,5,8,128]{3,2,1,0:T(8,128)S(1)}, f32[2,5,8,128]{3,2,1,0:T(8,128)S(1)}, u32[]{:S(2)}, u32[]{:S(2)}) %collective-permute-start.8) | collective-permute-done | bytes 40992 | tf_op jit(solution)/shard_map/ppermute | solution.py:430
  31.4 0.6 %collective-permute-done.9.refs_3_ = f32[2,5,8,128]{3,2,1,0:T(8,128)S(1)} collective-permute-done((f32[2,5,8,128]{3,2,1,0:T(8,128)S(1)}, f32[2,5,8,128]{3,2,1,0:T(8,128)S(1)}, u32[]{:S(2)}, u32[]{:S(2)}) %collective-permute-start.9) | collective-permute-done | bytes 40992 | tf_op jit(solution)/shard_map/ppermute | solution.py:430
  31.9 0.7 %unpack.1 = f32[2,5,32,128]{3,2,1,0:T(8,128)} custom-call(f32[2,5,8,128]{3,2,1,0:T(8,128)S(1)} %get-tuple-element.43.refs_0_, f32[2,5,8,128]{3,2,1,0:T(8,128)S(1)} %collective-permute-done.7.refs_1_, f32[2,5,8,128]{3,2,1,0:T(8,128)S(1)} %collective-permute-done.8.refs_2_, f32[2,5,8,128]{3,2,1,0:T(8,128)S(1)} %collective-permute-done.9.refs_3_), custom_call_target="tpu_custom_call" | custom-call | tf_op jit(solution)/shard_map/unpack/pallas_call | solution.py:507
  (5 shorter events, 0.0 us)
Async XLA Ops:
  1.4 8.2 %collective-permute-start.3 = (f32[656,128]{1,0:T(8,128)S(1)}, f32[656,128]{1,0:T(8,128)S(1)}, u32[]{:S(2)}, u32[]{:S(2)}) collective-permute-start(f32[656,128]{1,0:T(8,128)S(1)} %get-tuple-element.30), channel_id=1, source_target_pairs={{0,1},{1,0},{2,3},{3,2},{4,5},{5,4},{6,7},{7,6},{8,9},{9,8},{10,11... | collective-permute-start | bytes 1007624 | tf_op jit(solution)/shard_map/ppermute | solution.py:439
  1.9 7.9 %collective-permute-start = (f32[184,128]{1,0:T(8,128)S(1)}, f32[184,128]{1,0:T(8,128)S(1)}, u32[]{:S(2)}, u32[]{:S(2)}) collective-permute-start(f32[184,128]{1,0:T(8,128)S(1)} %get-tuple-element.27), channel_id=1, source_target_pairs={{0,24},{8,16},{16,8},{24,0},{1,25},{9,17},{17,9},{25,1},{2,26},{10... | collective-permute-start | bytes 282632 | tf_op jit(solution)/shard_map/ppermute | solution.py:430
  5.4 5.6 %collective-permute-start.1 = (f32[184,128]{1,0:T(8,128)S(1)}, f32[184,128]{1,0:T(8,128)S(1)}, u32[]{:S(2)}, u32[]{:S(2)}) collective-permute-start(f32[184,128]{1,0:T(8,128)S(1)} %get-tuple-element.28), channel_id=1, source_target_pairs={{0,8},{8,0},{16,24},{24,16},{1,9},{9,1},{17,25},{25,17},{2,10},{10... | collective-permute-start | bytes 282632 | tf_op jit(solution)/shard_map/ppermute | solution.py:430
  5.9 5.1 %collective-permute-start.2 = (f32[184,128]{1,0:T(8,128)S(1)}, f32[184,128]{1,0:T(8,128)S(1)}, u32[]{:S(2)}, u32[]{:S(2)}) collective-permute-start(f32[184,128]{1,0:T(8,128)S(1)} %get-tuple-element.29), channel_id=1, source_target_pairs={{0,16},{8,24},{16,0},{24,8},{1,17},{9,25},{17,1},{25,9},{2,18},{10... | collective-permute-start | bytes 282632 | tf_op jit(solution)/shard_map/ppermute | solution.py:430
  6.0 12.4 %collective-permute-start.4 = (f32[656,128]{1,0:T(8,128)S(1)}, f32[656,128]{1,0:T(8,128)S(1)}, u32[]{:S(2)}, u32[]{:S(2)}) collective-permute-start(f32[656,128]{1,0:T(8,128)S(1)} %get-tuple-element.40), channel_id=1, source_target_pairs={{1,2},{2,1},{3,4},{4,3},{5,6},{6,5},{0,8},{7,15},{9,10},{10,9},{11... | collective-permute-start | bytes 1007624 | tf_op jit(solution)/shard_map/ppermute | solution.py:438
  11.0 1.6 %collective-permute-start.6 = (f32[552,128]{1,0:T(8,128)S(1)}, f32[552,128]{1,0:T(8,128)S(1)}, u32[]{:S(2)}, u32[]{:S(2)}) collective-permute-start(f32[552,128]{1,0:T(8,128)S(1)} %constant_dynamic-update-slice_fusion), channel_id=1, source_target_pairs={{0,1},{1,0},{2,3},{3,2},{4,5},{5,4},{6,7},{7,6},{8,9},{9,8},{10,11... | collective-permute-start | bytes 847880 | tf_op jit(solution)/shard_map/ppermute | solution.py:475
  11.1 7.3 %collective-permute-start.5 = (f32[552,128]{1,0:T(8,128)S(1)}, f32[552,128]{1,0:T(8,128)S(1)}, u32[]{:S(2)}, u32[]{:S(2)}) collective-permute-start(f32[552,128]{1,0:T(8,128)S(1)} %constant_dynamic-update-slice_fusion), channel_id=1, source_target_pairs={{1,2},{2,1},{3,4},{4,3},{5,6},{6,5},{0,8},{7,15},{9,10},{10,9},{11... | collective-permute-start | bytes 847880 | tf_op jit(solution)/shard_map/ppermute | solution.py:474
  24.9 5.0 %collective-permute-start.7 = (f32[2,5,8,128]{3,2,1,0:T(8,128)S(1)}, f32[2,5,8,128]{3,2,1,0:T(8,128)S(1)}, u32[]{:S(2)}, u32[]{:S(2)}) collective-permute-start(f32[2,5,8,128]{3,2,1,0:T(8,128)S(1)} %get-tuple-element.44), channel_id=1, source_target_pairs={{0,24},{8,16},{16,8},{24,0},{1,25},{9,17},{17,9},{25,1},{2,26},{10... | collective-permute-start | bytes 122888 | tf_op jit(solution)/shard_map/ppermute | solution.py:430
  27.4 4.0 %collective-permute-start.8 = (f32[2,5,8,128]{3,2,1,0:T(8,128)S(1)}, f32[2,5,8,128]{3,2,1,0:T(8,128)S(1)}, u32[]{:S(2)}, u32[]{:S(2)}) collective-permute-start(f32[2,5,8,128]{3,2,1,0:T(8,128)S(1)} %get-tuple-element.45), channel_id=1, source_target_pairs={{0,8},{8,0},{16,24},{24,16},{1,9},{9,1},{17,25},{25,17},{2,10},{10... | collective-permute-start | bytes 122888 | tf_op jit(solution)/shard_map/ppermute | solution.py:430
  27.9 4.0 %collective-permute-start.9 = (f32[2,5,8,128]{3,2,1,0:T(8,128)S(1)}, f32[2,5,8,128]{3,2,1,0:T(8,128)S(1)}, u32[]{:S(2)}, u32[]{:S(2)}) collective-permute-start(f32[2,5,8,128]{3,2,1,0:T(8,128)S(1)} %get-tuple-element.46), channel_id=1, source_target_pairs={{0,16},{8,24},{16,0},{24,8},{1,17},{9,25},{17,1},{25,9},{2,18},{10... | collective-permute-start | bytes 122888 | tf_op jit(solution)/shard_map/ppermute | solution.py:430
